TPU v7x, 512 devices: a whole 4x8x8 slice. The times are simulated.
512 devices in a mesh: replica: 64 (over z_hi, y, core), tensor: 8 (over x, z_lo).
Axes of the slice: x: 4, y: 8, z: 8 (z_hi: 4, z_lo: 2; z = z_hi * 2 + z_lo), core: 2. Of those that a mesh axis runs over, the one named last changes fastest.
Arguments:
- queries: bfloat16 [2048, 8192], P('replica', 'tensor'), may hold values from -130 to 130
- cache_keys: bfloat16 [2048, 8, 128, 128], P('replica', 'tensor'), may hold values from -6 to 6
- cache_values: bfloat16 [2048, 8, 128, 128], P('replica', 'tensor'), may hold values from -6 to 6
- new_keys: bfloat16 [2048, 1024], P('replica', 'tensor'), may hold values from -6 to 6
- new_values: bfloat16 [2048, 1024], P('replica', 'tensor'), may hold values from -6 to 6
- cache_lengths: int32 [2048], P('replica'), may hold values from 2 to 128, as said below
- residual: bfloat16 [2048, 8192], P('replica', 'tensor'), may hold values from -90 to 90
- norm_gain: float32 [8192], P('tensor'), may hold values from 0.1 to 1.9
- draft_input: bfloat16 [2048, 8192], P('replica', 'tensor'), may hold values from -90 to 90
- trainer_of: int32 [64], P('replica'), may hold values from 0 to 15
- factor_down: float32 [64, 8192], P(None, 'tensor'), may hold values from -5 to 5
- factor_up: float32 [64, 8192], P(None, 'tensor'), may hold values from -5 to 5
Outputs:
- hidden_rows: bfloat16 [2048, 8192], P('replica', 'tensor')
- draft_next: bfloat16 [2048, 8192], P('replica', 'tensor')
- new_down: float32 [64, 8192], P(None, 'tensor')
- new_up: float32 [64, 8192], P(None, 'tensor')
Inputs may be any that keep to these rules, and one draw needn't show every extreme that they name: `cache_lengths`: every row has two or more live slots; some row has all 128.
All inputs are finite; a program needn't handle non-finite values.
Results may differ from a plain program's by a relative error of at most 0.0055.
Values sent between devices are 32-bit elements; how exact they have to be, the bound alone decides.
A program may use at most 64 MiB of HBM per device.

v0:
```python
import math

import jax
import jax.numpy as jnp
from jax import lax
from jax.sharding import PartitionSpec as P

D = 8192
RANK = 64


def attend_local(queries, cache_keys, cache_values, new_keys, new_values, cache_lengths):
    token_count, heads_here, slots, size = cache_keys.shape
    group = queries.shape[1] // (heads_here * size)
    score_scale = 1.0 / math.sqrt(size)
    query_r = queries.reshape(token_count, heads_here, group, size)
    scores = (
        jnp.einsum("bkgd,bkpd->bkgp", query_r, cache_keys, preferred_element_type=jnp.float32)
        * score_scale
    )
    own_scores = (
        jnp.einsum(
            "romy,roy->rom",
            query_r,
            new_keys.reshape(token_count, heads_here, size),
            preferred_element_type=jnp.float32,
        )
        * score_scale
    )
    live = jnp.arange(slots, dtype=jnp.int32)[None, :] < cache_lengths[:, None]
    scores = jnp.where(live[:, None, None, :], scores, -jnp.inf)
    top = jnp.maximum(jnp.max(scores, axis=-1), own_scores)
    weights = jnp.exp(scores - top[..., None])
    own_weight = jnp.exp(own_scores - top)
    total = jnp.sum(weights, axis=-1) + own_weight
    probs = (weights / total[..., None]).astype(jnp.bfloat16)
    own_prob = (own_weight / total).astype(jnp.bfloat16)
    context = jnp.einsum("bkgp,bkpd->bkgd", probs, cache_values, preferred_element_type=jnp.float32)
    context = context + own_prob.astype(jnp.float32)[..., None] * new_values.astype(
        jnp.float32
    ).reshape(token_count, heads_here, 1, size)
    return context.reshape(token_count, heads_here * group * size)


def local(
    queries,
    cache_keys,
    cache_values,
    new_keys,
    new_values,
    cache_lengths,
    residual,
    norm_gain,
    draft_input,
    trainer_of,
    factor_down,
    factor_up,
):
    rows_here = queries.shape[0]
    trainers = lax.axis_size("replica") // 4
    root_width = 1.0 / math.sqrt(D)
    coef = 0.5 / math.sqrt(RANK)
    onehot = (jnp.arange(trainers, dtype=jnp.int32) == trainer_of[0]).astype(jnp.float32)
    loads = lax.psum(onehot, "replica")
    down_b = factor_down.astype(jnp.bfloat16)
    up_b = factor_up.astype(jnp.bfloat16)
    adapter_part = jnp.dot(draft_input, down_b.T, preferred_element_type=jnp.float32)
    adapter_sum = lax.psum(adapter_part, "tensor")
    context = attend_local(queries, cache_keys, cache_values, new_keys, new_values, cache_lengths)
    feature = residual.astype(jnp.float32) + context
    square_part = jnp.sum(feature * feature, axis=1)
    square_sum = lax.psum(square_part, "tensor")
    mean_sq = (square_sum / D)[:, None]
    hidden_rows = (feature * lax.rsqrt(mean_sq + 1e-05) * norm_gain[None, :]).astype(jnp.bfloat16)
    adapter = (adapter_sum * root_width).astype(jnp.bfloat16)
    serve_part = jnp.dot(hidden_rows, down_b.T, preferred_element_type=jnp.float32)
    serve_sum = lax.psum(serve_part, "tensor")
    pred = draft_input.astype(jnp.float32) + coef * jnp.dot(
        adapter, up_b, preferred_element_type=jnp.float32
    )
    weight = 1.0 / (rows_here * jnp.sum(onehot * loads))
    resid_grad = (weight * (pred - hidden_rows.astype(jnp.float32))).astype(jnp.bfloat16)
    back_part = jnp.dot(resid_grad, up_b.T, preferred_element_type=jnp.float32)
    back_sum = lax.psum(back_part, "tensor")
    back = (coef * back_sum).astype(jnp.bfloat16)
    grad_up_local = coef * jnp.dot(adapter.T, resid_grad, preferred_element_type=jnp.float32)
    grad_down_local = jnp.dot(back.T, draft_input, preferred_element_type=jnp.float32) * root_width
    count_all = 2.0 * RANK * D
    grad_down, grad_up = lax.psum((grad_down_local, grad_up_local), "replica")
    total_sq = lax.psum(jnp.sum(grad_down * grad_down) + jnp.sum(grad_up * grad_up), "tensor")
    score_scale = jnp.sqrt(total_sq / count_all + 1e-06)
    new_down = factor_down - 0.5 * grad_down / score_scale
    new_up = factor_up - 0.5 * grad_up / score_scale
    serve = (serve_sum * root_width).astype(jnp.bfloat16)
    draft_next = (
        hidden_rows.astype(jnp.float32)
        + coef * jnp.dot(serve, up_b, preferred_element_type=jnp.float32)
    ).astype(jnp.bfloat16)
    return (hidden_rows, draft_next, new_down, new_up)


def solution(mesh):
    return jax.shard_map(
        local,
        mesh=mesh,
        in_specs=(
            P("replica", "tensor"),
            P("replica", "tensor", None, None),
            P("replica", "tensor", None, None),
            P("replica", "tensor"),
            P("replica", "tensor"),
            P("replica"),
            P("replica", "tensor"),
            P("tensor"),
            P("replica", "tensor"),
            P("replica"),
            P(None, "tensor"),
            P(None, "tensor"),
        ),
        out_specs=(
            P("replica", "tensor"),
            P("replica", "tensor"),
            P(None, "tensor"),
            P(None, "tensor"),
        ),
        check_vma=False,
    )
```

profile of v0, /device:TPU:1, one launch (start us, length us, event | category | flops | bytes accessed | tf_op | source)
XLA Modules:
  0.0 813.0 jit_solution(5041238318364325031)
XLA Ops:
  7.2 0.0 copy-start
  7.2 0.0 copy-start.8
  7.2 0.0 all-reduce.5.cloned.1.call-start
  8.0 145.7 %psum.58 = f32[16]{0:T(128)S(1)} all-reduce(f32[16]{0:T(128)S(1)} %compare_convert_fusion), channel_id=1, replica_groups=mesh['replica'=64,'tensor'=8] {'replica'}, use_global_device_ids=true, to_apply=%region_5.6 | all-reduce | flops 16 | bytes 128 | tf_op jit(solution)/shard_map/psum | solution.py:64
  153.7 0.7 iota_compare_fusion
  154.4 0.0 copy-done.8
  154.5 0.0 copy-start.11
  154.5 0.9 copy.18
  155.3 0.0 copy-start.10
  155.3 0.0 copy-done.11
  155.3 0.1 fusion.16
  155.5 0.0 copy-done
  155.5 0.0 copy-start.6
  155.5 0.7 fusion.31
  156.2 0.0 copy-start.2
  156.3 0.2 fusion.9
  156.5 0.0 copy-done.6
  156.5 0.7 copy-done.2
  157.2 0.1 fusion.10
  157.4 0.0 copy-done.10
  157.4 0.0 copy-start.7
  157.4 0.0 copy-start.9
  157.4 0.4 convolution_add_fusion
  157.8 0.0 copy-start.1
  157.9 0.4 copy-done.7
  158.2 0.1 multiply_reduce_fusion.2
  158.4 27.0 %all-reduce.2 = (f32[32]{0:T(128)S(1)}, f32[32,64]{1,0:T(8,128)S(1)}) all-reduce(f32[32]{0:T(128)S(1)} %multiply_reduce_fusion.2, f32[32,64]{1,0:T(8,128)S(1)} %fusion.10), channel_id=1, replica_groups=mesh['replica'=64,'tensor'=8] {'tensor'}, use_global_device_ids=true, to_apply=%region_3.4 | all-reduce | flops 2080 | bytes 16640 | tf_op jit(solution)/shard_map/psum | solution.py:72
  185.4 0.6 fusion.22
  186.7 0.0 copy-done.9
  186.7 0.1 multiply_convert_fusion
  186.8 0.0 copy-start.5
  186.8 0.0 copy-done.1
  186.8 0.2 fusion.5
  187.0 0.1 fusion.24
  187.1 0.9 convolution_multiply_fusion
  188.1 23.8 %psum.60 = f32[32,64]{1,0:T(8,128)S(1)} all-reduce(f32[32,64]{1,0:T(8,128)S(1)} %fusion.24), channel_id=1, replica_groups=mesh['replica'=64,'tensor'=8] {'tensor'}, use_global_device_ids=true, to_apply=%region_8.9 | all-reduce | flops 2048 | bytes 16384 | tf_op jit(solution)/shard_map/psum | solution.py:84
  211.9 0.9 convolution_multiply_fusion.1
  212.8 0.0 all-reduce.5.cloned.1.call-update
  212.8 0.1 fusion.12
  213.0 560.4 %all-reduce.5.cloned.1.call-done = (f32[64,1024]{1,0:T(8,128)}, f32[64,1024]{1,0:T(8,128)}) async-done(((f32[64,1024]{1,0:T(8,128)}, f32[64,1024]{1,0:T(8,128)}), (f32[64,1024]{1,0:T(8,128)}, f32[64,1024]{1,0:T(8,128)})) %all-reduce.5.cloned.1.call-update) | async-done | bytes 524304 | tf_op jit(solution)/shard_map/psum | solution.py:89
  773.4 0.0 copy-start.3
  773.4 0.0 copy-start.4
  773.4 1.7 multiply_reduce_fusion
  775.1 0.0 copy-done.3
  775.1 0.7 multiply_reduce_fusion.1
  777.0 26.8 %all-reduce.1 = (f32[32,64]{1,0:T(8,128)S(1)}, f32[]{:T(128)}) all-reduce(f32[32,64]{1,0:T(8,128)S(1)} %fusion.12, f32[]{:T(128)S(6)} %add.53), channel_id=1, replica_groups=mesh['replica'=64,'tensor'=8] {'tensor'}, use_global_device_ids=true, to_apply=%region_4.5 | all-reduce | flops 2049 | bytes 16392 | tf_op jit(solution)/shard_map/psum | solution.py:77
  804.5 0.0 copy-done.4
  804.5 0.9 divide_subtract_fusion
  805.4 0.0 copy-done.5
  805.4 0.8 fusion.6
  (5 shorter events, 0.0 us)
Async XLA Ops:
  7.2 148.3 %copy-start = (bf16[32,1,128,128]{3,2,1,0:T(8,128)(2,1)S(1)}, bf16[32,1,128,128]{3,2,1,0:T(8,128)(2,1)}, u32[]{:S(2)}) copy-start(bf16[32,1,128,128]{3,2,1,0:T(8,128)(2,1)} %param.13) | copy-start | bytes 3145732
  7.2 147.3 %copy-start.8 = (bf16[32,128]{1,0:T(8,128)(2,1)S(1)}, bf16[32,128]{1,0:T(8,128)(2,1)}, u32[]{:S(2)}) copy-start(bf16[32,128]{1,0:T(8,128)(2,1)} %param.16) | copy-start | bytes 24580
  7.2 766.2 %all-reduce.5.cloned.1.call-start = ((), (), s32[]{:S(2)}) async-start(), calls=%async_computation | async-start | bytes 1048576 | tf_op jit(solution)/shard_map/psum | solution.py:89
  154.5 0.9 copy-start.11
  155.3 2.0 copy-start.10
  155.5 1.0 copy-start.6
  156.2 1.0 copy-start.2
  157.4 0.8 copy-start.7
  157.4 29.3 %copy-start.9 = (f32[1024]{0:T(1024)S(1)}, f32[1024]{0:T(1024)}, u32[]{:S(2)}) copy-start(f32[1024]{0:T(1024)} %param.19) | copy-start | bytes 12292
  157.8 28.9 %copy-start.1 = (f32[64,1024]{1,0:T(8,128)S(1)}, f32[64,1024]{1,0:T(8,128)}, u32[]{:S(2)}) copy-start(f32[64,1024]{1,0:T(8,128)} %param.23) | copy-start | bytes 786436
  186.8 618.6 %copy-start.5 = (bf16[32,1024]{1,0:T(8,128)(2,1)}, bf16[32,1024]{1,0:T(8,128)(2,1)S(1)}, u32[]{:S(2)}) copy-start(bf16[32,1024]{1,0:T(8,128)(2,1)S(1)} %multiply_convert_fusion) | copy-start | bytes 196612
  773.4 1.7 copy-start.3
  773.4 31.1 %copy-start.4 = (f32[64,1024]{1,0:T(8,128)S(1)}, f32[64,1024]{1,0:T(8,128)}, u32[]{:S(2)}) copy-start(f32[64,1024]{1,0:T(8,128)} %get-tuple-element.5) | copy-start | bytes 786436
Sparse Core Ops, SparseCore 0:
  212.9 560.3 all-reduce.4
where the time goes:
time: 819 us; the launch traced here: 813 us
  waiting for transfers between devices  560 us (68%)
  blocking collectives  223 us (27%)
  between operations  17.6 us (2%)
    psum x1, waiting for transfers between devices, local(): grad_down, grad_up = lax.psum((grad_down_local, grad_up_local), 'replica')  560 us
    psum x1, blocking collectives, local(): loads = lax.psum(onehot, 'replica')  146 us
    psum x1, blocking collectives, local(): square_sum = lax.psum(square_part, 'tensor')  27 us
    psum x1, blocking collectives, local(): serve_sum = lax.psum(serve_part, 'tensor')  26.8 us
    psum x1, blocking collectives, local(): back_sum = lax.psum(back_part, 'tensor')  23.8 us
  transfers between devices with their start and end apart: 1, of which 1 were waited for; matrix products, arithmetic and copies ran while one was open for 0% of the time, Pallas kernels for 0%

commit v1 on v0

v1 whole, which is shorter than its diff:
```python
import functools
import math

import jax
import jax.numpy as jnp
from jax import lax
from jax.experimental import pallas as pl
from jax.experimental.pallas import tpu as pltpu
from jax.sharding import PartitionSpec as P

D = 8192
RANK = 64
ROWS = 32
GROUP = 8
SIZE = 128
WIDTH = 1024
NT = 8
NY = 8
NZ = 4
NYC = 16
ROOT = 1.0 / math.sqrt(D)
COEF = 0.5 / math.sqrt(RANK)
MESH = pl.DeviceIdType.MESH
BF = jnp.bfloat16
F32 = jnp.float32
EXACT = lax.Precision.HIGHEST


def iota(shape, dim):
    return lax.broadcasted_iota(jnp.int32, shape, dim)


def dot_t(a, b):
    return lax.dot_general(a, b, (((1,), (1,)), ((), ())), preferred_element_type=F32)


def dot_rows(a, b):
    return lax.dot_general(a, b, (((0,), (0,)), ((), ())), preferred_element_type=F32)


def remote(src, dst, send_sem, recv_sem, device):
    return pltpu.make_async_remote_copy(
        src_ref=src,
        dst_ref=dst,
        send_sem=send_sem,
        recv_sem=recv_sem,
        device_id=device,
        device_id_type=MESH,
    )


def kernel(
    q_hbm, ck_hbm, cv_hbm, nk_hbm, nv_hbm, len_hbm, res_hbm, gain_hbm, dr_hbm, tr_hbm, fd_hbm, fu_hbm,
    hid_hbm, dn_hbm, nd_hbm, nu_hbm,
    q_v, ck_v, cv_v, nk_v, nv_v, len_v, res_v, gain_v, dr_v, tr_v, fd_v, fu_v,
    hid_v, dn_v, nd_v, nu_v,
    w_b, q3, ctx3, fg_b,
    slices, t_buf, r_buf, x_buf, late, l_buf, c_buf, z_buf, grads, s_t, s_y,
    in_sem, out_sem,
    t_ss, t_rs, r_ss, r_rs, x_ss, x_rs, l_ss, l_rs, c_ss, c_rs, z_ss, z_rs, g_ss, g_rs, f_ss, f_rs,
    st_ss, st_rs, sy_ss, sy_rs,
):
    r = lax.axis_index("replica")
    t = lax.axis_index("tensor")
    yc = lax.rem(r, NYC)
    z = r // NYC
    y = yc // 2
    c = lax.rem(yc, 2)
    sibling = (z * NYC + y * 2 + (1 - c), t)
    t_peers = [lax.rem(t + o, NT) for o in range(1, NT)]
    yc_peers = [lax.rem(yc + o, NYC) for o in range(1, NYC)]
    z_peers = [lax.rem(z + o, NZ) for o in range(1, NZ)]
    y_peers = [lax.rem(y + o, NY) for o in range(1, NY)]

    barrier = pltpu.get_barrier_semaphore()
    everyone = (
        [(r, p) for p in t_peers]
        + [(z * NYC + p, t) for p in yc_peers]
        + [(p * NYC + yc, t) for p in z_peers]
    )
    for device in everyone:
        pl.semaphore_signal(barrier, inc=1, device_id=device, device_id_type=MESH)

    loads = [
        pltpu.make_async_copy(src, dst, in_sem.at[i])
        for i, (src, dst) in enumerate(
            (
                (fd_hbm, fd_v), (fu_hbm, fu_v), (dr_hbm, dr_v), (q_hbm, q_v), (nk_hbm, nk_v), (len_hbm, len_v),
                (ck_hbm, ck_v), (nv_hbm, nv_v), (res_hbm, res_v), (gain_hbm, gain_v), (tr_hbm, tr_v), (cv_hbm, cv_v),
            )
        )
    ]
    for load in loads:
        load.start()
    for load in loads[:3]:
        load.wait()

    w_b[0:RANK, :] = fd_v[...].astype(BF)
    w_b[RANK:, :] = fu_v[...].astype(BF)
    draft_part = dot_t(dr_v[...], w_b[...])
    up_part = dot_t(w_b[RANK:, :], w_b[...])
    for g in range(GROUP):
        slices[0, g] = dr_v[:, g * SIZE : (g + 1) * SIZE].astype(F32)

    for load in loads[3:6]:
        load.wait()
    for g in range(GROUP):
        q3[pl.ds(g, ROWS, stride=GROUP), :] = q_v[:, g * SIZE : (g + 1) * SIZE].astype(F32)
    pick = (iota((ROWS * GROUP, ROWS), 0) // GROUP == iota((ROWS * GROUP, ROWS), 1)).astype(F32)
    own_key = jnp.dot(pick.astype(BF), nk_v[...], preferred_element_type=F32)
    lengths = jnp.dot(
        (pick * len_v[...].astype(F32)).astype(BF), jnp.ones((ROWS, SIZE), BF), preferred_element_type=F32
    )
    queries = q3[...]
    scale = 1.0 / math.sqrt(SIZE)
    own_score = jnp.sum(queries * own_key, axis=1, keepdims=True) * scale
    loads[6].wait()
    scores = lax.dot_general(
        queries.reshape(ROWS, GROUP, SIZE).astype(BF),
        ck_v[...],
        (((2,), (2,)), ((0,), (0,))),
        preferred_element_type=F32,
    ).reshape(ROWS * GROUP, SIZE)
    live = iota((ROWS * GROUP, SIZE), 1).astype(F32) < lengths
    scores = jnp.where(live, scores * scale, -jnp.inf)
    top = jnp.maximum(jnp.max(scores, axis=1, keepdims=True), own_score)
    weights = jnp.exp(scores - top)
    own_weight = jnp.exp(own_score - top)
    total = jnp.sum(weights, axis=1, keepdims=True) + own_weight
    probs = (weights / total).astype(BF)
    own_prob = (own_weight / total).astype(BF).astype(F32)
    for load in loads[7:]:
        load.wait()
    own_value = jnp.dot(pick.astype(BF), nv_v[...], preferred_element_type=F32)
    context = lax.dot_general(
        probs.reshape(ROWS, GROUP, SIZE),
        cv_v[...],
        (((2,), (1,)), ((0,), (0,))),
        preferred_element_type=F32,
    ).reshape(ROWS * GROUP, SIZE)
    ctx3[...] = context + own_prob * own_value

    squares = jnp.zeros((ROWS, SIZE), F32)
    for g in range(GROUP):
        cols = slice(g * SIZE, (g + 1) * SIZE)
        feature = res_v[:, cols].astype(F32) + ctx3[pl.ds(g, ROWS, stride=GROUP), :]
        squares = squares + feature * feature
        gained = feature * gain_v[:, cols]
        slices[1, g] = gained
        fg_b[:, cols] = gained.astype(BF)
    square_col = jnp.sum(squares, axis=1, keepdims=True)
    eye = iota((ROWS, SIZE), 0) == iota((ROWS, SIZE), 1)
    square_row = jnp.sum(jnp.where(eye, square_col, 0.0), axis=0, keepdims=True)
    feature_part = dot_t(fg_b[...], w_b[...])
    low = iota((ROWS, SIZE), 1) < RANK

    t_buf[t, 0:32, :] = draft_part
    t_buf[t, 32:64, :] = jnp.where(low, feature_part, up_part[0:32])
    t_buf[t, 64:96, :] = jnp.where(low, pltpu.roll(feature_part, RANK, 1), up_part[32:64])
    t_buf[t, 96:104, :] = jnp.broadcast_to(square_row, (8, SIZE))
    onehot = (iota((1, SIZE), 1) == tr_v[...]).astype(F32)
    c_buf[z] = onehot
    r_buf[yc] = slices[c, y]

    pl.semaphore_wait(barrier, len(everyone))

    sent = []

    def send(src, dst, ss, rs, device):
        copy = remote(src, dst, ss, rs, device)
        copy.start()
        sent.append(copy)

    for i, p in enumerate(z_peers):
        send(c_buf.at[z], c_buf.at[z], c_ss.at[i], c_rs.at[z], (p * NYC + yc, t))
    for i, p in enumerate(t_peers):
        send(t_buf.at[t], t_buf.at[t], t_ss.at[i], t_rs.at[t], (r, p))
    for i, p in enumerate(yc_peers):
        send(slices.at[lax.rem(p, 2), p // 2], r_buf.at[yc], r_ss.at[i], r_rs.at[yc], (z * NYC + p, t))

    for i, p in enumerate(z_peers):
        remote(c_buf.at[p], c_buf.at[p], c_ss.at[i], c_rs.at[p], (p * NYC + yc, t)).wait_recv()
    counts = c_buf[0] + c_buf[1] + c_buf[2] + c_buf[3]
    for i, p in enumerate(t_peers):
        remote(t_buf.at[p], t_buf.at[p], t_ss.at[i], t_rs.at[p], (r, p)).wait_recv()
    summed = t_buf[0]
    for p in range(1, NT):
        summed = summed + t_buf[p]
    square_all = summed[96:97]
    rs_row = lax.rsqrt(square_all * (1.0 / D) + 1e-05)
    rs_col = jnp.sum(jnp.where(eye, rs_row, 0.0), axis=1, keepdims=True)
    adapter = (summed[0:32] * ROOT).astype(BF).astype(F32)
    spread = jnp.dot(adapter[:, 0:RANK], summed[32:96], precision=EXACT, preferred_element_type=F32)
    back = COEF * (summed[0:32] + COEF * spread - rs_col * pltpu.roll(summed[64:96], RANK, 1))
    low16 = low[0:16]
    row8 = iota((8, SIZE), 0)
    extra = jnp.where(row8 == 0, rs_row, jnp.where(row8 == 1, counts, jnp.where(row8 == 2, onehot, 0.0)))
    late[0, 0:16, :] = jnp.where(low16, pltpu.roll(back[0:16], RANK, 1), back[16:32])
    late[1, 0:16, :] = jnp.where(low16, adapter[0:16], pltpu.roll(adapter[16:32], RANK, 1))
    late[0, 16:24, :] = extra
    late[1, 16:24, :] = extra
    for i, p in enumerate(yc_peers):
        send(late.at[lax.rem(p, 2)], l_buf.at[yc], l_ss.at[i], l_rs.at[yc], (z * NYC + p, t))
    l_buf[yc] = late[c]

    serve = (summed[32:64] * rs_col * ROOT).astype(BF)
    drafted = jnp.dot(serve[:, 0:RANK], w_b[RANK:, :], preferred_element_type=F32)
    for g in range(GROUP):
        cols = slice(g * SIZE, (g + 1) * SIZE)
        hidden = (slices[1, g] * rs_col).astype(BF)
        hid_v[:, cols] = hidden
        dn_v[:, cols] = (hidden.astype(F32) + COEF * drafted[:, cols]).astype(BF)
    stores = [
        pltpu.make_async_copy(hid_v, hid_hbm, out_sem.at[0]),
        pltpu.make_async_copy(dn_v, dn_hbm, out_sem.at[1]),
    ]
    for store in stores:
        store.start()

    for i, p in enumerate(yc_peers):
        remote(r_buf.at[p], r_buf.at[p], r_ss.at[i], r_rs.at[p], (z * NYC + p, t)).wait_recv()
    swap = remote(r_buf, x_buf, x_ss, x_rs, sibling)
    swap.start()
    sent.append(swap)
    swap.wait_recv()
    for i, p in enumerate(yc_peers):
        remote(l_buf.at[p], l_buf.at[p], l_ss.at[i], l_rs.at[p], (z * NYC + p, t)).wait_recv()

    packed = l_buf[:, 0:16, :].reshape(256, SIZE)
    tiles = l_buf[:, 16:24, :]
    load_all = jnp.sum(tiles, axis=0)[1:2, :]
    tile_loads = jnp.sum(tiles * load_all[None], axis=2, keepdims=True)
    tile_loads = jnp.broadcast_to(tile_loads, (NYC, 8, SIZE)).reshape(SIZE, SIZE)
    first = (iota((256, SIZE), 0) // 16) * 8
    lane = iota((256, SIZE), 1)
    load_rows = jnp.dot(
        (lane == first + 2).astype(F32), tile_loads, precision=EXACT, preferred_element_type=F32
    )
    weight = 1.0 / (ROWS * load_rows)

    @pl.when(c == 0)
    def _():
        left = (packed * weight).astype(BF)
        top_rows = r_buf[:, 0:16, :].reshape(256, SIZE).astype(BF)
        bottom_rows = r_buf[:, 16:32, :].reshape(256, SIZE).astype(BF)
        z_buf[z] = (dot_rows(left, top_rows)[0:RANK] + dot_rows(left, bottom_rows)[RANK:]) * ROOT

    @pl.when(c == 1)
    def _():
        left = packed.astype(BF)
        up = w_b[RANK:, pl.ds(pl.multiple_of(y * SIZE, SIZE), SIZE)]
        none = jnp.zeros_like(up)
        rs_all = jnp.dot(
            (lane == first).astype(F32), tiles.reshape(SIZE, SIZE), precision=EXACT, preferred_element_type=F32
        )
        place = lax.rem(iota((256, SIZE), 0), 16)

        def half(h, up_half):
            rs = jnp.sum(jnp.where(lane == place + 16 * h, rs_all, 0.0), axis=1, keepdims=True)
            rows = slice(16 * h, 16 * h + 16)
            drafts = x_buf[:, rows, :].reshape(256, SIZE)
            gained = r_buf[:, rows, :].reshape(256, SIZE)
            lift = jnp.dot(left, up_half, preferred_element_type=F32)
            resid = (weight * (drafts + COEF * lift - rs * gained)).astype(BF)
            return dot_rows(left, resid)

        top_part = half(0, jnp.concatenate([up, none], axis=0))
        bottom_part = half(1, jnp.concatenate([none, up], axis=0))
        z_buf[z] = (top_part[0:RANK] + bottom_part[RANK:]) * COEF

    for i, p in enumerate(z_peers):
        send(z_buf.at[z], z_buf.at[z], z_ss.at[i], z_rs.at[z], (p * NYC + yc, t))
    for i, p in enumerate(z_peers):
        remote(z_buf.at[p], z_buf.at[p], z_ss.at[i], z_rs.at[p], (p * NYC + yc, t)).wait_recv()
    grad = z_buf[0] + z_buf[1] + z_buf[2] + z_buf[3]
    grads[c, y] = grad

    for i, p in enumerate(y_peers):
        send(grads.at[c, y], grads.at[c, y], g_ss.at[i], g_rs.at[y], (z * NYC + p * 2 + c, t))
    s_t[t] = jnp.sum(grad * grad, axis=0, keepdims=True)
    for i, p in enumerate(t_peers):
        send(s_t.at[t], s_t.at[t], st_ss.at[i], st_rs.at[t], (r, p))
    send(grads.at[c, y], grads.at[c, y], f_ss.at[y], f_rs.at[y], sibling)
    for i, p in enumerate(t_peers):
        remote(s_t.at[p], s_t.at[p], st_ss.at[i], st_rs.at[p], (r, p)).wait_recv()
    part = s_t[0]
    for p in range(1, NT):
        part = part + s_t[p]
    s_y[yc] = part
    for i, p in enumerate(yc_peers):
        send(s_y.at[yc], s_y.at[yc], sy_ss.at[i], sy_rs.at[yc], (z * NYC + p, t))
    for o in (1, 7, 2, 6, 3, 5, 4):
        p = lax.rem(y + o, NY)
        remote(grads.at[c, p], grads.at[c, p], g_ss.at[o - 1], g_rs.at[p], (z * NYC + p * 2 + c, t)).wait_recv()
        send(grads.at[c, p], grads.at[c, p], f_ss.at[p], f_rs.at[p], sibling)
    for i, p in enumerate(yc_peers):
        remote(s_y.at[p], s_y.at[p], sy_ss.at[i], sy_rs.at[p], (z * NYC + p, t)).wait_recv()
    whole = s_y[0]
    for p in range(1, NYC):
        whole = whole + s_y[p]
    total_sq = jnp.sum(whole, axis=1, keepdims=True)
    step = 0.5 / jnp.sqrt(total_sq * (1.0 / (2.0 * RANK * D)) + 1e-06)
    for p in range(NY):
        remote(grads.at[1 - c, p], grads.at[1 - c, p], f_ss.at[p], f_rs.at[p], sibling).wait_recv()
    for p in range(NY):
        cols = slice(p * SIZE, (p + 1) * SIZE)
        nd_v[:, cols] = fd_v[:, cols] - grads[0, p] * step
        nu_v[:, cols] = fu_v[:, cols] - grads[1, p] * step
    stores += [
        pltpu.make_async_copy(nd_v, nd_hbm, out_sem.at[2]),
        pltpu.make_async_copy(nu_v, nu_hbm, out_sem.at[3]),
    ]
    for store in stores[2:]:
        store.start()
    for copy in sent:
        copy.wait_send()
    for store in stores:
        store.wait()


def local(
    queries,
    cache_keys,
    cache_values,
    new_keys,
    new_values,
    cache_lengths,
    residual,
    norm_gain,
    draft_input,
    trainer_of,
    factor_down,
    factor_up,
):
    inputs = (
        queries,
        cache_keys.reshape(ROWS, SIZE, SIZE),
        cache_values.reshape(ROWS, SIZE, SIZE),
        new_keys,
        new_values,
        cache_lengths.reshape(1, ROWS),
        residual,
        norm_gain.reshape(1, WIDTH),
        draft_input,
        trainer_of.reshape(1, 1),
        factor_down,
        factor_up,
    )
    outs = (
        jax.ShapeDtypeStruct((ROWS, WIDTH), BF),
        jax.ShapeDtypeStruct((ROWS, WIDTH), BF),
        jax.ShapeDtypeStruct((RANK, WIDTH), F32),
        jax.ShapeDtypeStruct((RANK, WIDTH), F32),
    )
    vmem = pltpu.VMEM
    dma = pltpu.SemaphoreType.DMA
    scratch = (
        [vmem(a.shape, a.dtype) for a in inputs]
        + [vmem(a.shape, a.dtype) for a in outs]
        + [
            vmem((2 * RANK, WIDTH), BF),
            vmem((ROWS * GROUP, SIZE), F32),
            vmem((ROWS * GROUP, SIZE), F32),
            vmem((ROWS, WIDTH), BF),
            vmem((2, NY, ROWS, SIZE), F32),
            vmem((NT, 104, SIZE), F32),
            vmem((NYC, ROWS, SIZE), F32),
            vmem((NYC, ROWS, SIZE), F32),
            vmem((2, 24, SIZE), F32),
            vmem((NYC, 24, SIZE), F32),
            vmem((NZ, 1, SIZE), F32),
            vmem((NZ, RANK, SIZE), F32),
            vmem((2, NY, RANK, SIZE), F32),
            vmem((NT, 1, SIZE), F32),
            vmem((NYC, 1, SIZE), F32),
            dma((len(inputs),)),
            dma((len(outs),)),
            dma((NT - 1,)), dma((NT,)),
            dma((NYC - 1,)), dma((NYC,)),
            dma, dma,
            dma((NYC - 1,)), dma((NYC,)),
            dma((NZ - 1,)), dma((NZ,)),
            dma((NZ - 1,)), dma((NZ,)),
            dma((NY - 1,)), dma((NY,)),
            dma((NY,)), dma((NY,)),
            dma((NT - 1,)), dma((NT,)),
            dma((NYC - 1,)), dma((NYC,)),
        ]
    )
    anywhere = pl.BlockSpec(memory_space=pl.ANY)
    return pl.pallas_call(
        kernel,
        out_shape=outs,
        in_specs=[anywhere] * len(inputs),
        out_specs=tuple([anywhere] * len(outs)),
        scratch_shapes=scratch,
        compiler_params=pltpu.CompilerParams(
            collective_id=0, has_side_effects=True, vmem_limit_bytes=24 * 1024 * 1024
        ),
        name="decode_and_draft",
    )(*inputs)


def solution(mesh):
    return jax.shard_map(
        local,
        mesh=mesh,
        in_specs=(
            P("replica", "tensor"),
            P("replica", "tensor", None, None),
            P("replica", "tensor", None, None),
            P("replica", "tensor"),
            P("replica", "tensor"),
            P("replica"),
            P("replica", "tensor"),
            P("tensor"),
            P("replica", "tensor"),
            P("replica"),
            P(None, "tensor"),
            P(None, "tensor"),
        ),
        out_specs=(
            P("replica", "tensor"),
            P("replica", "tensor"),
            P(None, "tensor"),
            P(None, "tensor"),
        ),
        check_vma=False,
    )
```

time: 819 us -> 63.4 us (0.08)
  waiting for transfers between devices: 560 us -> 0 us
  blocking collectives: 223 us -> 0 us
  Pallas kernels: 0 us -> 49.9 us
  between operations: 17.6 us -> 1.33 us
  local copies, waits for them, and re-layouts: 2.03 us -> 11.6 us
    psum x1 -> x0, waiting for transfers between devices: 560 us -> none  [local(): grad_down, grad_up = lax.psum((grad_down_local, grad_up_local), 'replica')]
    psum x4 -> x0, blocking collectives: 223 us -> none  [the longest x1 146 us: local(): loads = lax.psum(onehot, 'replica')]
    pallas_call x0 -> x1, Pallas kernels: none -> 49.9 us  [local(): pl.pallas_call(kernel, out_shape=outs, in_specs=[anywhere] * len(inputs),...]
    unnamed x25 -> x26, local copies, waits for them, and re-layouts: 2.03 us -> 11.6 us
  transfers between devices with their start and end apart: 1 -> 0, of which waited for: 1 -> 0; matrix products, arithmetic and copies ran while one was open for 0% -> 0% of each run, Pallas kernels for 0% -> 0%
where the time goes in v1:
time: 63.4 us; the launch traced here: 62.8 us
  Pallas kernels  49.9 us (79%)
  local copies, waits for them, and re-layouts  11.6 us (18%)
  between operations  1.33 us (2%)
    pallas_call x1, Pallas kernels, local(): pl.pallas_call(kernel, out_shape=outs, in_specs=[anywhere] * len(inputs),...  49.9 us
    unnamed x26, local copies, waits for them, and re-layouts  11.6 us

profile of v1, /device:TPU:1, one launch (start us, length us, event | category | flops | bytes accessed | tf_op | source)
XLA Modules:
  0.0 62.8 jit_solution(1790002079233326613)
XLA Ops:
  0.6 0.0 copy-start.7
  1.3 0.0 copy-start.10
  1.3 0.0 copy-done.7
  1.3 0.6 copy-done.10
  2.0 0.0 copy-start
  2.0 1.2 %copy-done = bf16[32,1,128,128]{3,2,1,0:T(8,128)(2,1)S(1)} copy-done((bf16[32,1,128,128]{3,2,1,0:T(8,128)(2,1)S(1)}, bf16[32,1,128,128]{3,2,1,0:T(8,128)(2,1)}, u32[]{:S(2)}) %copy-start) | copy-done | bytes 1048600
  3.2 0.0 copy-start.1
  3.2 1.2 %copy-done.1 = bf16[32,1,128,128]{3,2,1,0:T(8,128)(2,1)S(1)} copy-done((bf16[32,1,128,128]{3,2,1,0:T(8,128)(2,1)S(1)}, bf16[32,1,128,128]{3,2,1,0:T(8,128)(2,1)}, u32[]{:S(2)}) %copy-start.1) | copy-done | bytes 1048600
  4.4 0.0 copy-start.2
  4.4 0.9 %copy-done.2 = f32[64,1024]{1,0:T(8,128)S(1)} copy-done((f32[64,1024]{1,0:T(8,128)S(1)}, f32[64,1024]{1,0:T(8,128)}, u32[]{:S(2)}) %copy-start.2) | copy-done | bytes 262168
  5.4 0.0 copy-start.3
  5.4 0.9 %copy-done.3 = f32[64,1024]{1,0:T(8,128)S(1)} copy-done((f32[64,1024]{1,0:T(8,128)S(1)}, f32[64,1024]{1,0:T(8,128)}, u32[]{:S(2)}) %copy-start.3) | copy-done | bytes 262168
  6.3 0.0 copy-start.4
  6.3 0.8 %copy-done.4 = bf16[32,1024]{1,0:T(8,128)(2,1)S(1)} copy-done((bf16[32,1024]{1,0:T(8,128)(2,1)S(1)}, bf16[32,1024]{1,0:T(8,128)(2,1)}, u32[]{:S(2)}) %copy-start.4) | copy-done | bytes 65560
  7.2 0.0 copy-start.5
  7.2 0.8 %copy-done.5 = bf16[32,1024]{1,0:T(8,128)(2,1)S(1)} copy-done((bf16[32,1024]{1,0:T(8,128)(2,1)S(1)}, bf16[32,1024]{1,0:T(8,128)(2,1)}, u32[]{:S(2)}) %copy-start.5) | copy-done | bytes 65560
  8.0 0.0 copy-start.6
  8.0 0.8 %copy-done.6 = bf16[32,1024]{1,0:T(8,128)(2,1)S(1)} copy-done((bf16[32,1024]{1,0:T(8,128)(2,1)S(1)}, bf16[32,1024]{1,0:T(8,128)(2,1)}, u32[]{:S(2)}) %copy-start.6) | copy-done | bytes 65560
  8.8 0.0 copy-start.8
  8.8 0.7 %copy-done.8 = bf16[32,128]{1,0:T(8,128)(2,1)S(1)} copy-done((bf16[32,128]{1,0:T(8,128)(2,1)S(1)}, bf16[32,128]{1,0:T(8,128)(2,1)}, u32[]{:S(2)}) %copy-start.8) | copy-done | bytes 8216
  9.5 0.0 copy-start.9
  9.5 0.7 %copy-done.9 = f32[1024]{0:T(1024)S(1)} copy-done((f32[1024]{0:T(1024)S(1)}, f32[1024]{0:T(1024)}, u32[]{:S(2)}) %copy-start.9) | copy-done | bytes 4120
  10.2 49.9 %decode_and_draft.1 = (bf16[32,1024]{1,0:T(8,128)(2,1)S(1)}, bf16[32,1024]{1,0:T(8,128)(2,1)S(1)}, f32[64,1024]{1,0:T(8,128)S(1)}, f32[64,1024]{1,0:T(8,128)S(1)}) custom-call(bf16[32,1024]{1,0:T(8,128)(2,1)S(1)} %copy-done.4, bf16[32,128,128]{2,1,0:T(8,128)(2,1)S(1)} %bitcast.6, bf16[32,128,128]{2,1,0:T(8,128)(2,1)S(1)} %bitcast.7, ...), custom_call_target="tpu_custom_call" | custom-call | tf_op jit(solution)/shard_map/decode_and_draft/pallas_call | solution.py:391
  60.2 0.6 %copy.21 = bf16[32,1024]{1,0:T(8,128)(2,1)} copy(bf16[32,1024]{1,0:T(8,128)(2,1)S(1)} %get-tuple-element.8) | data formatting | bytes 131072
  60.8 0.6 %copy.22 = bf16[32,1024]{1,0:T(8,128)(2,1)} copy(bf16[32,1024]{1,0:T(8,128)(2,1)S(1)} %get-tuple-element.9) | data formatting | bytes 131072
  61.4 0.7 %copy.23 = f32[64,1024]{1,0:T(8,128)} copy(f32[64,1024]{1,0:T(8,128)S(1)} %get-tuple-element.10) | data formatting | bytes 524288
  62.1 0.7 %copy.24 = f32[64,1024]{1,0:T(8,128)} copy(f32[64,1024]{1,0:T(8,128)S(1)} %get-tuple-element.11) | data formatting | bytes 524288
Async XLA Ops:
  0.6 0.7 %copy-start.7 = (bf16[32,128]{1,0:T(8,128)(2,1)S(1)}, bf16[32,128]{1,0:T(8,128)(2,1)}, u32[]{:S(2)}) copy-start(bf16[32,128]{1,0:T(8,128)(2,1)} %nk_hbm.1) | copy-start | bytes 24580
  1.3 0.7 %copy-start.10 = (s32[32]{0:T(128)S(1)}, s32[32]{0:T(128)}, u32[]{:S(2)}) copy-start(s32[32]{0:T(128)} %param.17) | copy-start | bytes 388
  2.0 1.2 %copy-start = (bf16[32,1,128,128]{3,2,1,0:T(8,128)(2,1)S(1)}, bf16[32,1,128,128]{3,2,1,0:T(8,128)(2,1)}, u32[]{:S(2)}) copy-start(bf16[32,1,128,128]{3,2,1,0:T(8,128)(2,1)} %param.13) | copy-start | bytes 3145732
  3.2 1.2 %copy-start.1 = (bf16[32,1,128,128]{3,2,1,0:T(8,128)(2,1)S(1)}, bf16[32,1,128,128]{3,2,1,0:T(8,128)(2,1)}, u32[]{:S(2)}) copy-start(bf16[32,1,128,128]{3,2,1,0:T(8,128)(2,1)} %param.14) | copy-start | bytes 3145732
  4.4 0.9 %copy-start.2 = (f32[64,1024]{1,0:T(8,128)S(1)}, f32[64,1024]{1,0:T(8,128)}, u32[]{:S(2)}) copy-start(f32[64,1024]{1,0:T(8,128)} %fd_hbm.1) | copy-start | bytes 786436
  5.4 0.9 %copy-start.3 = (f32[64,1024]{1,0:T(8,128)S(1)}, f32[64,1024]{1,0:T(8,128)}, u32[]{:S(2)}) copy-start(f32[64,1024]{1,0:T(8,128)} %fu_hbm.1) | copy-start | bytes 786436
  6.3 0.8 %copy-start.4 = (bf16[32,1024]{1,0:T(8,128)(2,1)S(1)}, bf16[32,1024]{1,0:T(8,128)(2,1)}, u32[]{:S(2)}) copy-start(bf16[32,1024]{1,0:T(8,128)(2,1)} %q_hbm.1) | copy-start | bytes 196612
  7.2 0.8 %copy-start.5 = (bf16[32,1024]{1,0:T(8,128)(2,1)S(1)}, bf16[32,1024]{1,0:T(8,128)(2,1)}, u32[]{:S(2)}) copy-start(bf16[32,1024]{1,0:T(8,128)(2,1)} %res_hbm.1) | copy-start | bytes 196612
  8.0 0.8 %copy-start.6 = (bf16[32,1024]{1,0:T(8,128)(2,1)S(1)}, bf16[32,1024]{1,0:T(8,128)(2,1)}, u32[]{:S(2)}) copy-start(bf16[32,1024]{1,0:T(8,128)(2,1)} %dr_hbm.1) | copy-start | bytes 196612
  8.8 0.7 %copy-start.8 = (bf16[32,128]{1,0:T(8,128)(2,1)S(1)}, bf16[32,128]{1,0:T(8,128)(2,1)}, u32[]{:S(2)}) copy-start(bf16[32,128]{1,0:T(8,128)(2,1)} %nv_hbm.1) | copy-start | bytes 24580
  9.5 0.7 %copy-start.9 = (f32[1024]{0:T(1024)S(1)}, f32[1024]{0:T(1024)}, u32[]{:S(2)}) copy-start(f32[1024]{0:T(1024)} %param.19) | copy-start | bytes 12292

commit v2 on v1

--- a/solution.py
+++ b/solution.py
@@ -56,9 +56,7 @@
     hid_v, dn_v, nd_v, nu_v,
     w_b, q3, ctx3, fg_b,
     slices, t_buf, r_buf, x_buf, late, l_buf, c_buf, z_buf, grads, s_t, s_y,
-    in_sem, out_sem,
-    t_ss, t_rs, r_ss, r_rs, x_ss, x_rs, l_ss, l_rs, c_ss, c_rs, z_ss, z_rs, g_ss, g_rs, f_ss, f_rs,
-    st_ss, st_rs, sy_ss, sy_rs,
+    in_sem, out_sem, send_sem, recv_sem, slice_sem,
 ):
     r = lax.axis_index("replica")
     t = lax.axis_index("tensor")
@@ -66,17 +64,35 @@
     z = r // NYC
     y = yc // 2
     c = lax.rem(yc, 2)
-    sibling = (z * NYC + y * 2 + (1 - c), t)
-    t_peers = [lax.rem(t + o, NT) for o in range(1, NT)]
-    yc_peers = [lax.rem(yc + o, NYC) for o in range(1, NYC)]
-    z_peers = [lax.rem(z + o, NZ) for o in range(1, NZ)]
-    y_peers = [lax.rem(y + o, NY) for o in range(1, NY)]
+    x = t // 2
+    low_z = lax.rem(t, 2)
+    y_order = (4, 3, 5, 2, 6, 1, 7)
+    t_peers = [
+        lax.rem(x + dx, 4) * 2 + lax.rem(low_z + dz, 2)
+        for dx, dz in ((2, 1), (1, 1), (3, 1), (2, 0), (1, 0), (3, 0), (0, 1))
+    ]
+    yc_peers = [lax.rem(y + dy, NY) * 2 + lax.rem(c + dc, 2) for dy in y_order for dc in (0, 1)]
+    yc_peers = yc_peers + [y * 2 + 1 - c]
+    z_peers = [lax.rem(z + dz, NZ) for dz in (2, 1, 3)]
+    y_peers = [lax.rem(y + dy, NY) for dy in y_order]
+
+    def at_t(p):
+        return (r, p)
+
+    def at_yc(p):
+        return (z * NYC + p, t)
+
+    def at_z(p):
+        return (p * NYC + yc, t)
+
+    sibling = at_yc(y * 2 + 1 - c)
 
     barrier = pltpu.get_barrier_semaphore()
     everyone = (
-        [(r, p) for p in t_peers]
-        + [(z * NYC + p, t) for p in yc_peers]
-        + [(p * NYC + yc, t) for p in z_peers]
+        [at_t(p) for p in t_peers]
+        + [at_yc(p) for p in yc_peers]
+        + [at_z(p) for p in z_peers]
+        + [(z * NYC + y * 2 + 1 - c, p) for p in t_peers]
     )
     for device in everyone:
         pl.semaphore_signal(barrier, inc=1, device_id=device, device_id_type=MESH)
@@ -158,31 +174,38 @@
     t_buf[t, 32:64, :] = jnp.where(low, feature_part, up_part[0:32])
     t_buf[t, 64:96, :] = jnp.where(low, pltpu.roll(feature_part, RANK, 1), up_part[32:64])
     t_buf[t, 96:104, :] = jnp.broadcast_to(square_row, (8, SIZE))
-    onehot = (iota((1, SIZE), 1) == tr_v[...]).astype(F32)
+    onehot = (iota((1, SIZE), 1) == tr_v[...] + 64).astype(F32)
     c_buf[z] = onehot
     r_buf[yc] = slices[c, y]
 
     pl.semaphore_wait(barrier, len(everyone))
 
-    sent = []
-
-    def send(src, dst, ss, rs, device):
-        copy = remote(src, dst, ss, rs, device)
-        copy.start()
-        sent.append(copy)
-
-    for i, p in enumerate(z_peers):
-        send(c_buf.at[z], c_buf.at[z], c_ss.at[i], c_rs.at[z], (p * NYC + yc, t))
-    for i, p in enumerate(t_peers):
-        send(t_buf.at[t], t_buf.at[t], t_ss.at[i], t_rs.at[t], (r, p))
-    for i, p in enumerate(yc_peers):
-        send(slices.at[lax.rem(p, 2), p // 2], r_buf.at[yc], r_ss.at[i], r_rs.at[yc], (z * NYC + p, t))
-
-    for i, p in enumerate(z_peers):
-        remote(c_buf.at[p], c_buf.at[p], c_ss.at[i], c_rs.at[p], (p * NYC + yc, t)).wait_recv()
+    drains = []
+
+    def spread_to(phase, devices, src, dst, size):
+        for i, device in enumerate(devices):
+            remote(src(i), dst, send_sem.at[phase], recv_sem.at[phase], device).start()
+        drains.append((phase, size))
+
+    def arrived(phase, size):
+        remote(size, size, send_sem.at[phase], recv_sem.at[phase], sibling).wait_recv()
+
+    t_size = t_buf.at[pl.ds(0, NT - 1)]
+    c_size = c_buf.at[pl.ds(0, NZ - 1)]
+    r_size = r_buf.at[pl.ds(0, NYC - 1)]
+    spread_to(0, [at_t(p) for p in t_peers], lambda i: t_buf.at[t], t_buf.at[t], t_size)
+    spread_to(1, [at_z(p) for p in z_peers], lambda i: c_buf.at[z], c_buf.at[z], c_size)
+    spread_to(
+        2,
+        [at_yc(p) for p in yc_peers],
+        lambda i: slices.at[lax.rem(yc_peers[i], 2), yc_peers[i] // 2],
+        r_buf.at[yc],
+        r_size,
+    )
+
+    arrived(1, c_size)
     counts = c_buf[0] + c_buf[1] + c_buf[2] + c_buf[3]
-    for i, p in enumerate(t_peers):
-        remote(t_buf.at[p], t_buf.at[p], t_ss.at[i], t_rs.at[p], (r, p)).wait_recv()
+    arrived(0, t_size)
     summed = t_buf[0]
     for p in range(1, NT):
         summed = summed + t_buf[p]
@@ -193,15 +216,20 @@
     spread = jnp.dot(adapter[:, 0:RANK], summed[32:96], precision=EXACT, preferred_element_type=F32)
     back = COEF * (summed[0:32] + COEF * spread - rs_col * pltpu.roll(summed[64:96], RANK, 1))
     low16 = low[0:16]
-    row8 = iota((8, SIZE), 0)
-    extra = jnp.where(row8 == 0, rs_row, jnp.where(row8 == 1, counts, jnp.where(row8 == 2, onehot, 0.0)))
+    extra = jnp.where(iota((1, SIZE), 1) < ROWS, rs_row, 0.0) + onehot + pltpu.roll(counts, 32, 1)
     late[0, 0:16, :] = jnp.where(low16, pltpu.roll(back[0:16], RANK, 1), back[16:32])
     late[1, 0:16, :] = jnp.where(low16, adapter[0:16], pltpu.roll(adapter[16:32], RANK, 1))
-    late[0, 16:24, :] = extra
-    late[1, 16:24, :] = extra
-    for i, p in enumerate(yc_peers):
-        send(late.at[lax.rem(p, 2)], l_buf.at[yc], l_ss.at[i], l_rs.at[yc], (z * NYC + p, t))
-    l_buf[yc] = late[c]
+    late[0, 16:17, :] = extra
+    late[1, 16:17, :] = extra
+    l_size = l_buf.at[pl.ds(0, NYC - 1), pl.ds(0, 17)]
+    spread_to(
+        3,
+        [at_yc(p) for p in yc_peers],
+        lambda i: late.at[lax.rem(yc_peers[i], 2), pl.ds(0, 17)],
+        l_buf.at[yc, pl.ds(0, 17)],
+        l_size,
+    )
+    l_buf[yc, 0:17, :] = late[c, 0:17, :]
 
     serve = (summed[32:64] * rs_col * ROOT).astype(BF)
     drafted = jnp.dot(serve[:, 0:RANK], w_b[RANK:, :], preferred_element_type=F32)
@@ -217,26 +245,21 @@
     for store in stores:
         store.start()
 
-    for i, p in enumerate(yc_peers):
-        remote(r_buf.at[p], r_buf.at[p], r_ss.at[i], r_rs.at[p], (z * NYC + p, t)).wait_recv()
-    swap = remote(r_buf, x_buf, x_ss, x_rs, sibling)
-    swap.start()
-    sent.append(swap)
-    swap.wait_recv()
-    for i, p in enumerate(yc_peers):
-        remote(l_buf.at[p], l_buf.at[p], l_ss.at[i], l_rs.at[p], (z * NYC + p, t)).wait_recv()
+    arrived(2, r_size)
+    remote(r_buf, x_buf, send_sem.at[4], recv_sem.at[4], sibling).start()
+    drains.append((4, r_buf))
+    arrived(4, r_buf)
+    arrived(3, l_size)
 
     packed = l_buf[:, 0:16, :].reshape(256, SIZE)
     tiles = l_buf[:, 16:24, :]
-    load_all = jnp.sum(tiles, axis=0)[1:2, :]
-    tile_loads = jnp.sum(tiles * load_all[None], axis=2, keepdims=True)
-    tile_loads = jnp.broadcast_to(tile_loads, (NYC, 8, SIZE)).reshape(SIZE, SIZE)
-    first = (iota((256, SIZE), 0) // 16) * 8
+    tiles = jnp.where(iota((NYC, 8, SIZE), 1) == 0, tiles, 0.0)
     lane = iota((256, SIZE), 1)
-    load_rows = jnp.dot(
-        (lane == first + 2).astype(F32), tile_loads, precision=EXACT, preferred_element_type=F32
-    )
-    weight = 1.0 / (ROWS * load_rows)
+    load_all = pltpu.roll(jnp.sum(jnp.sum(tiles, axis=0), axis=0, keepdims=True), 96, 1)
+    load_all = jnp.where(iota((1, SIZE), 1) // 16 == 4, load_all, 0.0)
+    own_row = (lane == (iota((256, SIZE), 0) // 16) * 8).astype(F32)
+    extras = jnp.dot(own_row, tiles.reshape(SIZE, SIZE), precision=EXACT, preferred_element_type=F32)
+    weight = 1.0 / (ROWS * jnp.sum(extras * load_all, axis=1, keepdims=True))
 
     @pl.when(c == 0)
     def _():
@@ -250,13 +273,10 @@
         left = packed.astype(BF)
         up = w_b[RANK:, pl.ds(pl.multiple_of(y * SIZE, SIZE), SIZE)]
         none = jnp.zeros_like(up)
-        rs_all = jnp.dot(
-            (lane == first).astype(F32), tiles.reshape(SIZE, SIZE), precision=EXACT, preferred_element_type=F32
-        )
         place = lax.rem(iota((256, SIZE), 0), 16)
 
         def half(h, up_half):
-            rs = jnp.sum(jnp.where(lane == place + 16 * h, rs_all, 0.0), axis=1, keepdims=True)
+            rs = jnp.sum(jnp.where(lane == place + 16 * h, extras, 0.0), axis=1, keepdims=True)
             rows = slice(16 * h, 16 * h + 16)
             drafts = x_buf[:, rows, :].reshape(256, SIZE)
             gained = r_buf[:, rows, :].reshape(256, SIZE)
@@ -268,40 +288,48 @@
         bottom_part = half(1, jnp.concatenate([none, up], axis=0))
         z_buf[z] = (top_part[0:RANK] + bottom_part[RANK:]) * COEF
 
-    for i, p in enumerate(z_peers):
-        send(z_buf.at[z], z_buf.at[z], z_ss.at[i], z_rs.at[z], (p * NYC + yc, t))
-    for i, p in enumerate(z_peers):
-        remote(z_buf.at[p], z_buf.at[p], z_ss.at[i], z_rs.at[p], (p * NYC + yc, t)).wait_recv()
+    z_size = z_buf.at[pl.ds(0, NZ - 1)]
+    spread_to(5, [at_z(p) for p in z_peers], lambda i: z_buf.at[z], z_buf.at[z], z_size)
+    arrived(5, z_size)
     grad = z_buf[0] + z_buf[1] + z_buf[2] + z_buf[3]
     grads[c, y] = grad
 
-    for i, p in enumerate(y_peers):
-        send(grads.at[c, y], grads.at[c, y], g_ss.at[i], g_rs.at[y], (z * NYC + p * 2 + c, t))
-    s_t[t] = jnp.sum(grad * grad, axis=0, keepdims=True)
-    for i, p in enumerate(t_peers):
-        send(s_t.at[t], s_t.at[t], st_ss.at[i], st_rs.at[t], (r, p))
-    send(grads.at[c, y], grads.at[c, y], f_ss.at[y], f_rs.at[y], sibling)
-    for i, p in enumerate(t_peers):
-        remote(s_t.at[p], s_t.at[p], st_ss.at[i], st_rs.at[p], (r, p)).wait_recv()
-    part = s_t[0]
-    for p in range(1, NT):
-        part = part + s_t[p]
-    s_y[yc] = part
-    for i, p in enumerate(yc_peers):
-        send(s_y.at[yc], s_y.at[yc], sy_ss.at[i], sy_rs.at[yc], (z * NYC + p, t))
-    for o in (1, 7, 2, 6, 3, 5, 4):
-        p = lax.rem(y + o, NY)
-        remote(grads.at[c, p], grads.at[c, p], g_ss.at[o - 1], g_rs.at[p], (z * NYC + p * 2 + c, t)).wait_recv()
-        send(grads.at[c, p], grads.at[c, p], f_ss.at[p], f_rs.at[p], sibling)
-    for i, p in enumerate(yc_peers):
-        remote(s_y.at[p], s_y.at[p], sy_ss.at[i], sy_rs.at[p], (z * NYC + p, t)).wait_recv()
-    whole = s_y[0]
-    for p in range(1, NYC):
-        whole = whole + s_y[p]
+    s_y[y] = jnp.sum(grad * grad, axis=0, keepdims=True)
+    own_core = [at_yc(p * 2 + c) for p in y_peers]
+    s_size = s_y.at[pl.ds(0, NY - 1)]
+    spread_to(6, own_core, lambda i: s_y.at[y], s_y.at[y], s_size)
+    mine = grads.at[c, y]
+    for device in own_core:
+        remote(mine, mine, send_sem.at[7], slice_sem.at[y], device).start()
+    g_size = grads.at[0, pl.ds(0, NY - 1)]
+    drains.append((7, g_size))
+    remote(mine, mine, send_sem.at[8], recv_sem.at[8], sibling).start()
+    arrived(6, s_size)
+    part = s_y[0]
+    for p in range(1, NY):
+        part = part + s_y[p]
+    place_t = t * 2 + c
+    s_t[place_t] = part
+    st_size = s_t.at[pl.ds(0, 2 * NT - 1)]
+    spread_to(
+        9,
+        [at_t(p) for p in t_peers] + [(z * NYC + y * 2 + 1 - c, p) for p in t_peers] + [sibling],
+        lambda i: s_t.at[place_t],
+        s_t.at[place_t],
+        st_size,
+    )
+    for p in reversed(y_peers):
+        piece = grads.at[c, p]
+        remote(piece, piece, send_sem.at[7], slice_sem.at[p], sibling).wait_recv()
+        remote(piece, piece, send_sem.at[8], recv_sem.at[8], sibling).start()
+    drains.append((8, grads.at[0]))
+    arrived(9, st_size)
+    whole = s_t[0]
+    for p in range(1, 2 * NT):
+        whole = whole + s_t[p]
     total_sq = jnp.sum(whole, axis=1, keepdims=True)
     step = 0.5 / jnp.sqrt(total_sq * (1.0 / (2.0 * RANK * D)) + 1e-06)
-    for p in range(NY):
-        remote(grads.at[1 - c, p], grads.at[1 - c, p], f_ss.at[p], f_rs.at[p], sibling).wait_recv()
+    arrived(8, grads.at[0])
     for p in range(NY):
         cols = slice(p * SIZE, (p + 1) * SIZE)
         nd_v[:, cols] = fd_v[:, cols] - grads[0, p] * step
@@ -312,10 +340,19 @@
     ]
     for store in stores[2:]:
         store.start()
-    for copy in sent:
-        copy.wait_send()
+    for phase, size in drains:
+        remote(size, size, send_sem.at[phase], recv_sem.at[phase], sibling).wait_send()
     for store in stores:
         store.wait()
+
+
+def hand_over(*refs):
+    *refs, sem = refs
+    copies = [pltpu.make_async_copy(refs[i], refs[4 + i], sem.at[i]) for i in (2, 3, 0, 1)]
+    for copy in copies:
+        copy.start()
+    for copy in copies:
+        copy.wait()
 
 
 def local(
@@ -371,34 +408,38 @@
             vmem((NZ, 1, SIZE), F32),
             vmem((NZ, RANK, SIZE), F32),
             vmem((2, NY, RANK, SIZE), F32),
-            vmem((NT, 1, SIZE), F32),
-            vmem((NYC, 1, SIZE), F32),
+            vmem((2 * NT, 1, SIZE), F32),
+            vmem((NY, 1, SIZE), F32),
             dma((len(inputs),)),
             dma((len(outs),)),
-            dma((NT - 1,)), dma((NT,)),
-            dma((NYC - 1,)), dma((NYC,)),
-            dma, dma,
-            dma((NYC - 1,)), dma((NYC,)),
-            dma((NZ - 1,)), dma((NZ,)),
-            dma((NZ - 1,)), dma((NZ,)),
-            dma((NY - 1,)), dma((NY,)),
-            dma((NY,)), dma((NY,)),
-            dma((NT - 1,)), dma((NT,)),
-            dma((NYC - 1,)), dma((NYC,)),
+            dma((10,)),
+            dma((10,)),
+            dma((NY,)),
         ]
     )
     anywhere = pl.BlockSpec(memory_space=pl.ANY)
-    return pl.pallas_call(
+    results = pl.pallas_call(
         kernel,
         out_shape=outs,
         in_specs=[anywhere] * len(inputs),
         out_specs=tuple([anywhere] * len(outs)),
         scratch_shapes=scratch,
         compiler_params=pltpu.CompilerParams(
-            collective_id=0, has_side_effects=True, vmem_limit_bytes=24 * 1024 * 1024
+            collective_id=0, has_side_effects=True, vmem_limit_bytes=60 * 1024 * 1024
         ),
         name="decode_and_draft",
     )(*inputs)
+    return tuple(
+        pl.pallas_call(
+            hand_over,
+            out_shape=outs,
+            in_specs=[anywhere] * len(outs),
+            out_specs=tuple([anywhere] * len(outs)),
+            scratch_shapes=[dma((len(outs),))],
+            compiler_params=pltpu.CompilerParams(vmem_limit_bytes=60 * 1024 * 1024),
+            name="hand_over",
+        )(*results)
+    )
 
 
 def solution(mesh):

time: 63.4 us -> 68.3 us (1.077)
  Pallas kernels: 49.9 us -> 66.8 us
  local copies, waits for them, and re-layouts: 11.6 us -> 0 us
    pallas_call x0 -> x1, Pallas kernels: none -> 21 us  [local(): pl.pallas_call(hand_over, out_shape=outs, in_specs=[anywhere] * len(outs)...]
    unnamed x26 -> x0, local copies, waits for them, and re-layouts: 11.6 us -> none
    pallas_call x1, Pallas kernels: 49.9 us -> 45.8 us  [local(): pl.pallas_call(kernel, out_shape=outs, in_specs=[anywhere] * len(inputs),...]
where the time goes in v2:
time: 68.3 us; the launch traced here: 68.1 us
  Pallas kernels  66.8 us (98%)
  between operations  1.29 us (2%)
    pallas_call x1, Pallas kernels, local(): pl.pallas_call(kernel, out_shape=outs, in_specs=[anywhere] * len(inputs),...  45.8 us
    pallas_call x1, Pallas kernels, local(): pl.pallas_call(hand_over, out_shape=outs, in_specs=[anywhere] * len(outs)...  21 us

profile of v2, /device:TPU:1, one launch (start us, length us, event | category | flops | bytes accessed | tf_op | source)
XLA Modules:
  0.0 68.1 jit_solution(4369614748384775536)
XLA Ops:
  1.3 45.8 %decode_and_draft.1 = (bf16[32,1024]{1,0:T(8,128)(2,1)}, bf16[32,1024]{1,0:T(8,128)(2,1)}, f32[64,1024]{1,0:T(8,128)}, f32[64,1024]{1,0:T(8,128)}) custom-call(bf16[32,1024]{1,0:T(8,128)(2,1)} %q_hbm.1, bf16[32,128,128]{2,1,0:T(8,128)(2,1)} %bitcast.6, bf16[32,128,128]{2,1,0:T(8,128)(2,1)} %bitcast.7, bf16[32,128]{1,0:T(8,128)(2,1)} %nk_hbm.1, ...), custom_call_target="tpu_custom_call" | custom-call | tf_op jit(solution)/shard_map/decode_and_draft/pallas_call | solution.py:421
  47.1 21.0 %hand_over.1 = (bf16[32,1024]{1,0:T(8,128)(2,1)}, bf16[32,1024]{1,0:T(8,128)(2,1)}, f32[64,1024]{1,0:T(8,128)}, f32[64,1024]{1,0:T(8,128)}) custom-call(bf16[32,1024]{1,0:T(8,128)(2,1)} %get-tuple-element.8.refs_0_, bf16[32,1024]{1,0:T(8,128)(2,1)} %get-tuple-element.9.refs_1_, f32[64,1024]{1,0:T(8,128)} %get-tuple-element.10.refs_2_, ...), custom_call_target="tpu_custom_call" | custom-call | tf_op jit(solution)/shard_map/hand_over/pallas_call | solution.py:433

commit v3 on v2

--- a/solution.py
+++ b/solution.py
@@ -51,12 +51,11 @@
 
 def kernel(
     q_hbm, ck_hbm, cv_hbm, nk_hbm, nv_hbm, len_hbm, res_hbm, gain_hbm, dr_hbm, tr_hbm, fd_hbm, fu_hbm,
-    hid_hbm, dn_hbm, nd_hbm, nu_hbm,
+    hid_v, dn_v, nd_v, nu_v,
     q_v, ck_v, cv_v, nk_v, nv_v, len_v, res_v, gain_v, dr_v, tr_v, fd_v, fu_v,
-    hid_v, dn_v, nd_v, nu_v,
     w_b, q3, ctx3, fg_b,
     slices, t_buf, r_buf, x_buf, late, l_buf, c_buf, z_buf, grads, s_t, s_y,
-    in_sem, out_sem, send_sem, recv_sem, slice_sem,
+    in_sem, send_sem, recv_sem, slice_sem,
 ):
     r = lax.axis_index("replica")
     t = lax.axis_index("tensor")
@@ -238,12 +237,6 @@
         hidden = (slices[1, g] * rs_col).astype(BF)
         hid_v[:, cols] = hidden
         dn_v[:, cols] = (hidden.astype(F32) + COEF * drafted[:, cols]).astype(BF)
-    stores = [
-        pltpu.make_async_copy(hid_v, hid_hbm, out_sem.at[0]),
-        pltpu.make_async_copy(dn_v, dn_hbm, out_sem.at[1]),
-    ]
-    for store in stores:
-        store.start()
 
     arrived(2, r_size)
     remote(r_buf, x_buf, send_sem.at[4], recv_sem.at[4], sibling).start()
@@ -334,16 +327,8 @@
         cols = slice(p * SIZE, (p + 1) * SIZE)
         nd_v[:, cols] = fd_v[:, cols] - grads[0, p] * step
         nu_v[:, cols] = fu_v[:, cols] - grads[1, p] * step
-    stores += [
-        pltpu.make_async_copy(nd_v, nd_hbm, out_sem.at[2]),
-        pltpu.make_async_copy(nu_v, nu_hbm, out_sem.at[3]),
-    ]
-    for store in stores[2:]:
-        store.start()
     for phase, size in drains:
         remote(size, size, send_sem.at[phase], recv_sem.at[phase], sibling).wait_send()
-    for store in stores:
-        store.wait()
 
 
 def hand_over(*refs):
@@ -393,7 +378,6 @@
     dma = pltpu.SemaphoreType.DMA
     scratch = (
         [vmem(a.shape, a.dtype) for a in inputs]
-        + [vmem(a.shape, a.dtype) for a in outs]
         + [
             vmem((2 * RANK, WIDTH), BF),
             vmem((ROWS * GROUP, SIZE), F32),
@@ -411,7 +395,6 @@
             vmem((2 * NT, 1, SIZE), F32),
             vmem((NY, 1, SIZE), F32),
             dma((len(inputs),)),
-            dma((len(outs),)),
             dma((10,)),
             dma((10,)),
             dma((NY,)),
@@ -420,9 +403,9 @@
     anywhere = pl.BlockSpec(memory_space=pl.ANY)
     results = pl.pallas_call(
         kernel,
-        out_shape=outs,
+        out_shape=tuple(vmem(a.shape, a.dtype) for a in outs),
         in_specs=[anywhere] * len(inputs),
-        out_specs=tuple([anywhere] * len(outs)),
+        out_specs=tuple([pl.BlockSpec(memory_space=vmem)] * len(outs)),
         scratch_shapes=scratch,
         compiler_params=pltpu.CompilerParams(
             collective_id=0, has_side_effects=True, vmem_limit_bytes=60 * 1024 * 1024
@@ -433,10 +416,9 @@
         pl.pallas_call(
             hand_over,
             out_shape=outs,
-            in_specs=[anywhere] * len(outs),
+            in_specs=[pl.BlockSpec(memory_space=vmem)] * len(outs),
             out_specs=tuple([anywhere] * len(outs)),
             scratch_shapes=[dma((len(outs),))],
-            compiler_params=pltpu.CompilerParams(vmem_limit_bytes=60 * 1024 * 1024),
             name="hand_over",
         )(*results)
     )

time: 68.3 us -> 51.1 us (0.75)
  Pallas kernels: 66.8 us -> 47 us
  local copies, waits for them, and re-layouts: 0 us -> 2.63 us
    pallas_call x2, Pallas kernels: 66.8 us -> 47 us  [the longest x1 45.1 us: local(): pl.pallas_call(kernel, out_shape=tuple((vmem(a.shape, a.dtype) for a in o...]
    unnamed x0 -> x8, local copies, waits for them, and re-layouts: none -> 2.63 us
where the time goes in v3:
time: 51.1 us; the launch traced here: 51 us
  Pallas kernels  47 us (92%)
  local copies, waits for them, and re-layouts  2.63 us (5%)
  between operations  1.3 us (3%)
    pallas_call x1, Pallas kernels, local(): pl.pallas_call(kernel, out_shape=tuple((vmem(a.shape, a.dtype) for a in o...  45.1 us
    unnamed x8, local copies, waits for them, and re-layouts  2.63 us
    pallas_call x1, Pallas kernels, local(): pl.pallas_call(hand_over, out_shape=outs, in_specs=[pl.BlockSpec(memory_s...  1.96 us

profile of v3, /device:TPU:1, one launch (start us, length us, event | category | flops | bytes accessed | tf_op | source)
XLA Modules:
  0.0 51.0 jit_solution(7328342927032689948)
XLA Ops:
  1.3 45.1 %decode_and_draft.1 = (bf16[32,1024]{1,0:T(8,128)(2,1)S(1)}, bf16[32,1024]{1,0:T(8,128)(2,1)S(1)}, f32[64,1024]{1,0:T(8,128)S(1)}, f32[64,1024]{1,0:T(8,128)S(1)}) custom-call(bf16[32,1024]{1,0:T(8,128)(2,1)} %q_hbm.1, bf16[32,128,128]{2,1,0:T(8,128)(2,1)} %bitcast.6, bf16[32,128,128]{2,1,0:T(8,128)(2,1)} %bitcast.7, bf16[32,128]{1,0:T(8,128)(2,1)} %nk_hbm.1, ...), custom_call_target="tpu_custom_call" | custom-call | tf_op jit(solution)/shard_map/decode_and_draft/pallas_call | solution.py:404
  46.4 0.0 copy-start
  46.4 0.7 %copy-done = f32[64,1024]{1,0:T(8,128)} copy-done((f32[64,1024]{1,0:T(8,128)}, f32[64,1024]{1,0:T(8,128)S(1)}, u32[]{:S(2)}) %copy-start) | copy-done | bytes 262168
  47.1 0.0 copy-start.1
  47.1 0.7 %copy-done.1 = f32[64,1024]{1,0:T(8,128)} copy-done((f32[64,1024]{1,0:T(8,128)}, f32[64,1024]{1,0:T(8,128)S(1)}, u32[]{:S(2)}) %copy-start.1) | copy-done | bytes 262168
  47.8 0.0 copy-start.2
  47.8 0.6 %copy-done.2 = bf16[32,1024]{1,0:T(8,128)(2,1)} copy-done((bf16[32,1024]{1,0:T(8,128)(2,1)}, bf16[32,1024]{1,0:T(8,128)(2,1)S(1)}, u32[]{:S(2)}) %copy-start.2) | copy-done | bytes 65560
  48.4 0.0 copy-start.3
  48.4 0.6 %copy-done.3 = bf16[32,1024]{1,0:T(8,128)(2,1)} copy-done((bf16[32,1024]{1,0:T(8,128)(2,1)}, bf16[32,1024]{1,0:T(8,128)(2,1)S(1)}, u32[]{:S(2)}) %copy-start.3) | copy-done | bytes 65560
  49.0 2.0 %hand_over.1 = (bf16[32,1024]{1,0:T(8,128)(2,1)}, bf16[32,1024]{1,0:T(8,128)(2,1)}, f32[64,1024]{1,0:T(8,128)}, f32[64,1024]{1,0:T(8,128)}) custom-call(bf16[32,1024]{1,0:T(8,128)(2,1)} %copy-done.2, bf16[32,1024]{1,0:T(8,128)(2,1)} %copy-done.3, f32[64,1024]{1,0:T(8,128)} %copy-done, f32[64,1024]{1,0:T(8,128)} %copy-done.1), custom_call_target="tpu_custom_call" | custom-call | tf_op jit(solution)/shard_map/hand_over/pallas_call | solution.py:416
Async XLA Ops:
  46.4 0.7 %copy-start = (f32[64,1024]{1,0:T(8,128)}, f32[64,1024]{1,0:T(8,128)S(1)}, u32[]{:S(2)}) copy-start(f32[64,1024]{1,0:T(8,128)S(1)} %get-tuple-element.10.refs_2_) | copy-start | bytes 786436
  47.1 0.7 %copy-start.1 = (f32[64,1024]{1,0:T(8,128)}, f32[64,1024]{1,0:T(8,128)S(1)}, u32[]{:S(2)}) copy-start(f32[64,1024]{1,0:T(8,128)S(1)} %get-tuple-element.11.refs_3_) | copy-start | bytes 786436
  47.8 0.6 %copy-start.2 = (bf16[32,1024]{1,0:T(8,128)(2,1)}, bf16[32,1024]{1,0:T(8,128)(2,1)S(1)}, u32[]{:S(2)}) copy-start(bf16[32,1024]{1,0:T(8,128)(2,1)S(1)} %get-tuple-element.8.refs_0_) | copy-start | bytes 196612
  48.4 0.6 %copy-start.3 = (bf16[32,1024]{1,0:T(8,128)(2,1)}, bf16[32,1024]{1,0:T(8,128)(2,1)S(1)}, u32[]{:S(2)}) copy-start(bf16[32,1024]{1,0:T(8,128)(2,1)S(1)} %get-tuple-element.9.refs_1_) | copy-start | bytes 196612

commit v4 on v3

--- a/solution.py
+++ b/solution.py
@@ -54,7 +54,7 @@
     hid_v, dn_v, nd_v, nu_v,
     q_v, ck_v, cv_v, nk_v, nv_v, len_v, res_v, gain_v, dr_v, tr_v, fd_v, fu_v,
     w_b, q3, ctx3, fg_b,
-    slices, t_buf, r_buf, x_buf, late, l_buf, c_buf, z_buf, grads, s_t, s_y,
+    slices, e_buf, f_buf, r_buf, x_buf, a_buf, l_buf, base, c_buf, z_buf, grads, s_t, s_y,
     in_sem, send_sem, recv_sem, slice_sem,
 ):
     r = lax.axis_index("replica")
@@ -100,24 +100,14 @@
         pltpu.make_async_copy(src, dst, in_sem.at[i])
         for i, (src, dst) in enumerate(
             (
-                (fd_hbm, fd_v), (fu_hbm, fu_v), (dr_hbm, dr_v), (q_hbm, q_v), (nk_hbm, nk_v), (len_hbm, len_v),
-                (ck_hbm, ck_v), (nv_hbm, nv_v), (res_hbm, res_v), (gain_hbm, gain_v), (tr_hbm, tr_v), (cv_hbm, cv_v),
+                (q_hbm, q_v), (nk_hbm, nk_v), (len_hbm, len_v), (tr_hbm, tr_v), (ck_hbm, ck_v), (fd_hbm, fd_v),
+                (fu_hbm, fu_v), (dr_hbm, dr_v), (cv_hbm, cv_v), (nv_hbm, nv_v), (res_hbm, res_v), (gain_hbm, gain_v),
             )
         )
     ]
     for load in loads:
         load.start()
-    for load in loads[:3]:
-        load.wait()
-
-    w_b[0:RANK, :] = fd_v[...].astype(BF)
-    w_b[RANK:, :] = fu_v[...].astype(BF)
-    draft_part = dot_t(dr_v[...], w_b[...])
-    up_part = dot_t(w_b[RANK:, :], w_b[...])
-    for g in range(GROUP):
-        slices[0, g] = dr_v[:, g * SIZE : (g + 1) * SIZE].astype(F32)
-
-    for load in loads[3:6]:
+    for load in loads[:4]:
         load.wait()
     for g in range(GROUP):
         q3[pl.ds(g, ROWS, stride=GROUP), :] = q_v[:, g * SIZE : (g + 1) * SIZE].astype(F32)
@@ -129,13 +119,27 @@
     queries = q3[...]
     scale = 1.0 / math.sqrt(SIZE)
     own_score = jnp.sum(queries * own_key, axis=1, keepdims=True) * scale
-    loads[6].wait()
+    loads[4].wait()
     scores = lax.dot_general(
         queries.reshape(ROWS, GROUP, SIZE).astype(BF),
         ck_v[...],
         (((2,), (2,)), ((0,), (0,))),
         preferred_element_type=F32,
     ).reshape(ROWS * GROUP, SIZE)
+
+    for load in loads[5:8]:
+        load.wait()
+    low = iota((ROWS, SIZE), 1) < RANK
+    w_b[0:RANK, :] = fd_v[...].astype(BF)
+    w_b[RANK:, :] = fu_v[...].astype(BF)
+    for g in range(GROUP):
+        slices[0, g] = dr_v[:, g * SIZE : (g + 1) * SIZE].astype(F32)
+    e_buf[t, 0:32, :] = dot_t(dr_v[...], w_b[...])
+    up_part = dot_t(w_b[RANK:, :], w_b[...])
+    e_buf[t, 32:64, :] = jnp.where(low, pltpu.roll(up_part[0:32], RANK, 1), up_part[32:64])
+    onehot = (iota((1, SIZE), 1) == tr_v[...] + 64).astype(F32)
+    c_buf[z] = onehot
+
     live = iota((ROWS * GROUP, SIZE), 1).astype(F32) < lengths
     scores = jnp.where(live, scores * scale, -jnp.inf)
     top = jnp.maximum(jnp.max(scores, axis=1, keepdims=True), own_score)
@@ -144,7 +148,31 @@
     total = jnp.sum(weights, axis=1, keepdims=True) + own_weight
     probs = (weights / total).astype(BF)
     own_prob = (own_weight / total).astype(BF).astype(F32)
-    for load in loads[7:]:
+
+    pl.semaphore_wait(barrier, len(everyone))
+    drains = []
+
+    def start(phase, src, dst, device):
+        remote(src, dst, send_sem.at[phase], recv_sem.at[phase], device).start()
+
+    def spread_to(phase, devices, src, size):
+        for device in devices:
+            start(phase, src, src, device)
+        drains.append((phase, size))
+
+    def arrived(phase, size):
+        remote(size, size, send_sem.at[phase], recv_sem.at[phase], sibling).wait_recv()
+
+    e_size = e_buf.at[pl.ds(0, NT - 1)]
+    f_size = f_buf.at[pl.ds(0, NT - 1), pl.ds(0, 33)]
+    c_size = c_buf.at[pl.ds(0, NZ - 1)]
+    r_size = r_buf.at[pl.ds(0, NYC - 1)]
+    spread_to(0, [at_t(p) for p in t_peers], e_buf.at[t], e_size)
+    spread_to(1, [at_z(p) for p in z_peers], c_buf.at[z], c_size)
+    for p in y_peers:
+        start(2, slices.at[0, p], r_buf.at[yc], at_yc(p * 2))
+
+    for load in loads[8:]:
         load.wait()
     own_value = jnp.dot(pick.astype(BF), nv_v[...], preferred_element_type=F32)
     context = lax.dot_general(
@@ -167,70 +195,58 @@
     eye = iota((ROWS, SIZE), 0) == iota((ROWS, SIZE), 1)
     square_row = jnp.sum(jnp.where(eye, square_col, 0.0), axis=0, keepdims=True)
     feature_part = dot_t(fg_b[...], w_b[...])
-    low = iota((ROWS, SIZE), 1) < RANK
-
-    t_buf[t, 0:32, :] = draft_part
-    t_buf[t, 32:64, :] = jnp.where(low, feature_part, up_part[0:32])
-    t_buf[t, 64:96, :] = jnp.where(low, pltpu.roll(feature_part, RANK, 1), up_part[32:64])
-    t_buf[t, 96:104, :] = jnp.broadcast_to(square_row, (8, SIZE))
-    onehot = (iota((1, SIZE), 1) == tr_v[...] + 64).astype(F32)
-    c_buf[z] = onehot
+    f_buf[t, 0:32, :] = feature_part
+    f_buf[t, 32:33, :] = square_row
+    spread_to(3, [at_t(p) for p in t_peers], f_buf.at[t, pl.ds(0, 33)], f_size)
+    for p in y_peers:
+        start(2, slices.at[1, p], r_buf.at[yc], at_yc(p * 2 + 1))
+    start(2, slices.at[1 - c, y], r_buf.at[yc], sibling)
+    drains.append((2, r_size))
     r_buf[yc] = slices[c, y]
 
-    pl.semaphore_wait(barrier, len(everyone))
-
-    drains = []
-
-    def spread_to(phase, devices, src, dst, size):
-        for i, device in enumerate(devices):
-            remote(src(i), dst, send_sem.at[phase], recv_sem.at[phase], device).start()
-        drains.append((phase, size))
-
-    def arrived(phase, size):
-        remote(size, size, send_sem.at[phase], recv_sem.at[phase], sibling).wait_recv()
-
-    t_size = t_buf.at[pl.ds(0, NT - 1)]
-    c_size = c_buf.at[pl.ds(0, NZ - 1)]
-    r_size = r_buf.at[pl.ds(0, NYC - 1)]
-    spread_to(0, [at_t(p) for p in t_peers], lambda i: t_buf.at[t], t_buf.at[t], t_size)
-    spread_to(1, [at_z(p) for p in z_peers], lambda i: c_buf.at[z], c_buf.at[z], c_size)
-    spread_to(
-        2,
-        [at_yc(p) for p in yc_peers],
-        lambda i: slices.at[lax.rem(yc_peers[i], 2), yc_peers[i] // 2],
-        r_buf.at[yc],
-        r_size,
-    )
-
+    arrived(0, e_size)
+    early = e_buf[0]
+    for p in range(1, NT):
+        early = early + e_buf[p]
+    low16 = low[0:16]
+    adapter = (early[0:32] * ROOT).astype(BF).astype(F32)
+    a_buf[yc] = jnp.where(low16, adapter[0:16], pltpu.roll(adapter[16:32], RANK, 1))
+    for p in y_peers:
+        start(4, a_buf.at[yc], a_buf.at[yc], at_yc(p * 2 + 1))
+    start(4, a_buf.at[yc], a_buf.at[yc], sibling)
+    drains.append((4, a_buf.at[pl.ds(0, NY)]))
+    ups = early[32:64]
+    upper = jnp.dot(adapter[:, 0:32], ups, precision=EXACT, preferred_element_type=F32)
+    lower = jnp.dot(pltpu.roll(adapter, 96, 1)[:, 0:32], ups, precision=EXACT, preferred_element_type=F32)
+    ahead = early[0:32] + COEF * (pltpu.roll(upper, RANK, 1) + lower)
     arrived(1, c_size)
     counts = c_buf[0] + c_buf[1] + c_buf[2] + c_buf[3]
-    arrived(0, t_size)
-    summed = t_buf[0]
+    marks = onehot + pltpu.roll(counts, 32, 1)
+    arrived(3, f_size)
+    summed = f_buf[0, 0:33, :]
     for p in range(1, NT):
-        summed = summed + t_buf[p]
-    square_all = summed[96:97]
-    rs_row = lax.rsqrt(square_all * (1.0 / D) + 1e-05)
+        summed = summed + f_buf[p, 0:33, :]
+    rs_row = lax.rsqrt(summed[32:33] * (1.0 / D) + 1e-05)
     rs_col = jnp.sum(jnp.where(eye, rs_row, 0.0), axis=1, keepdims=True)
-    adapter = (summed[0:32] * ROOT).astype(BF).astype(F32)
-    spread = jnp.dot(adapter[:, 0:RANK], summed[32:96], precision=EXACT, preferred_element_type=F32)
-    back = COEF * (summed[0:32] + COEF * spread - rs_col * pltpu.roll(summed[64:96], RANK, 1))
-    low16 = low[0:16]
-    extra = jnp.where(iota((1, SIZE), 1) < ROWS, rs_row, 0.0) + onehot + pltpu.roll(counts, 32, 1)
-    late[0, 0:16, :] = jnp.where(low16, pltpu.roll(back[0:16], RANK, 1), back[16:32])
-    late[1, 0:16, :] = jnp.where(low16, adapter[0:16], pltpu.roll(adapter[16:32], RANK, 1))
-    late[0, 16:17, :] = extra
-    late[1, 16:17, :] = extra
-    l_size = l_buf.at[pl.ds(0, NYC - 1), pl.ds(0, 17)]
-    spread_to(
-        3,
-        [at_yc(p) for p in yc_peers],
-        lambda i: late.at[lax.rem(yc_peers[i], 2), pl.ds(0, 17)],
-        l_buf.at[yc, pl.ds(0, 17)],
-        l_size,
-    )
-    l_buf[yc, 0:17, :] = late[c, 0:17, :]
-
-    serve = (summed[32:64] * rs_col * ROOT).astype(BF)
+    back = COEF * (ahead - rs_col * summed[0:32])
+    l_buf[yc, 0:16, :] = jnp.where(low16, pltpu.roll(back[0:16], RANK, 1), back[16:32])
+    l_buf[yc, 16:17, :] = jnp.where(iota((1, SIZE), 1) < ROWS, rs_row, 0.0) + marks
+    l_mine = l_buf.at[yc, pl.ds(0, 17)]
+    l_row = l_buf.at[yc, pl.ds(16, 1)]
+    for p in y_peers:
+        start(5, l_mine, l_mine, at_yc(p * 2))
+        start(6, l_row, l_row, at_yc(p * 2 + 1))
+    start(5, l_mine, l_mine, sibling)
+    drains.append((5, l_buf.at[pl.ds(0, NY), pl.ds(0, 17)]))
+    drains.append((6, l_buf.at[pl.ds(0, NY - 1), pl.ds(16, 1)]))
+
+    arrived(2, r_size)
+
+    @pl.when(c == 0)
+    def _():
+        start(7, r_buf, x_buf, sibling)
+
+    serve = (summed[0:32] * rs_col * ROOT).astype(BF)
     drafted = jnp.dot(serve[:, 0:RANK], w_b[RANK:, :], preferred_element_type=F32)
     for g in range(GROUP):
         cols = slice(g * SIZE, (g + 1) * SIZE)
@@ -238,13 +254,25 @@
         hid_v[:, cols] = hidden
         dn_v[:, cols] = (hidden.astype(F32) + COEF * drafted[:, cols]).astype(BF)
 
-    arrived(2, r_size)
-    remote(r_buf, x_buf, send_sem.at[4], recv_sem.at[4], sibling).start()
-    drains.append((4, r_buf))
-    arrived(4, r_buf)
-    arrived(3, l_size)
-
-    packed = l_buf[:, 0:16, :].reshape(256, SIZE)
+    @pl.when(c == 0)
+    def _():
+        arrived(4, a_buf.at[0])
+        arrived(5, l_buf.at[pl.ds(0, NYC - 1), pl.ds(0, 17)])
+
+    @pl.when(c == 1)
+    def _():
+        arrived(4, a_buf.at[pl.ds(0, NYC - 1)])
+        left = a_buf[...].reshape(256, SIZE).astype(BF)
+        up = w_b[RANK:, pl.ds(pl.multiple_of(y * SIZE, SIZE), SIZE)]
+        none = jnp.zeros_like(up)
+        lift_top = jnp.dot(left, jnp.concatenate([up, none], axis=0), preferred_element_type=F32)
+        lift_bottom = jnp.dot(left, jnp.concatenate([none, up], axis=0), preferred_element_type=F32)
+        arrived(7, x_buf)
+        base[0] = x_buf[:, 0:16, :].reshape(256, SIZE) + COEF * lift_top
+        base[1] = x_buf[:, 16:32, :].reshape(256, SIZE) + COEF * lift_bottom
+        arrived(5, l_buf.at[0, pl.ds(0, 17)])
+        arrived(6, l_buf.at[pl.ds(0, NYC - 2), pl.ds(16, 1)])
+
     tiles = l_buf[:, 16:24, :]
     tiles = jnp.where(iota((NYC, 8, SIZE), 1) == 0, tiles, 0.0)
     lane = iota((256, SIZE), 1)
@@ -256,48 +284,40 @@
 
     @pl.when(c == 0)
     def _():
-        left = (packed * weight).astype(BF)
+        left = (l_buf[:, 0:16, :].reshape(256, SIZE) * weight).astype(BF)
         top_rows = r_buf[:, 0:16, :].reshape(256, SIZE).astype(BF)
         bottom_rows = r_buf[:, 16:32, :].reshape(256, SIZE).astype(BF)
         z_buf[z] = (dot_rows(left, top_rows)[0:RANK] + dot_rows(left, bottom_rows)[RANK:]) * ROOT
 
     @pl.when(c == 1)
     def _():
-        left = packed.astype(BF)
-        up = w_b[RANK:, pl.ds(pl.multiple_of(y * SIZE, SIZE), SIZE)]
-        none = jnp.zeros_like(up)
+        left = a_buf[...].reshape(256, SIZE).astype(BF)
         place = lax.rem(iota((256, SIZE), 0), 16)
 
-        def half(h, up_half):
+        def half(h):
             rs = jnp.sum(jnp.where(lane == place + 16 * h, extras, 0.0), axis=1, keepdims=True)
-            rows = slice(16 * h, 16 * h + 16)
-            drafts = x_buf[:, rows, :].reshape(256, SIZE)
-            gained = r_buf[:, rows, :].reshape(256, SIZE)
-            lift = jnp.dot(left, up_half, preferred_element_type=F32)
-            resid = (weight * (drafts + COEF * lift - rs * gained)).astype(BF)
-            return dot_rows(left, resid)
-
-        top_part = half(0, jnp.concatenate([up, none], axis=0))
-        bottom_part = half(1, jnp.concatenate([none, up], axis=0))
-        z_buf[z] = (top_part[0:RANK] + bottom_part[RANK:]) * COEF
+            gained = r_buf[:, 16 * h : 16 * h + 16, :].reshape(256, SIZE)
+            return dot_rows(left, (weight * (base[h] - rs * gained)).astype(BF))
+
+        z_buf[z] = (half(0)[0:RANK] + half(1)[RANK:]) * COEF
 
     z_size = z_buf.at[pl.ds(0, NZ - 1)]
-    spread_to(5, [at_z(p) for p in z_peers], lambda i: z_buf.at[z], z_buf.at[z], z_size)
-    arrived(5, z_size)
+    spread_to(8, [at_z(p) for p in z_peers], z_buf.at[z], z_size)
+    arrived(8, z_size)
     grad = z_buf[0] + z_buf[1] + z_buf[2] + z_buf[3]
     grads[c, y] = grad
 
     s_y[y] = jnp.sum(grad * grad, axis=0, keepdims=True)
     own_core = [at_yc(p * 2 + c) for p in y_peers]
     s_size = s_y.at[pl.ds(0, NY - 1)]
-    spread_to(6, own_core, lambda i: s_y.at[y], s_y.at[y], s_size)
+    spread_to(9, own_core, s_y.at[y], s_size)
     mine = grads.at[c, y]
     for device in own_core:
-        remote(mine, mine, send_sem.at[7], slice_sem.at[y], device).start()
+        remote(mine, mine, send_sem.at[10], slice_sem.at[y], device).start()
     g_size = grads.at[0, pl.ds(0, NY - 1)]
-    drains.append((7, g_size))
-    remote(mine, mine, send_sem.at[8], recv_sem.at[8], sibling).start()
-    arrived(6, s_size)
+    drains.append((10, g_size))
+    start(11, mine, mine, sibling)
+    arrived(9, s_size)
     part = s_y[0]
     for p in range(1, NY):
         part = part + s_y[p]
@@ -305,30 +325,33 @@
     s_t[place_t] = part
     st_size = s_t.at[pl.ds(0, 2 * NT - 1)]
     spread_to(
-        9,
+        12,
         [at_t(p) for p in t_peers] + [(z * NYC + y * 2 + 1 - c, p) for p in t_peers] + [sibling],
-        lambda i: s_t.at[place_t],
         s_t.at[place_t],
         st_size,
     )
     for p in reversed(y_peers):
         piece = grads.at[c, p]
-        remote(piece, piece, send_sem.at[7], slice_sem.at[p], sibling).wait_recv()
-        remote(piece, piece, send_sem.at[8], recv_sem.at[8], sibling).start()
-    drains.append((8, grads.at[0]))
-    arrived(9, st_size)
+        remote(piece, piece, send_sem.at[10], slice_sem.at[p], sibling).wait_recv()
+        start(11, piece, piece, sibling)
+    drains.append((11, grads.at[0]))
+    arrived(12, st_size)
     whole = s_t[0]
     for p in range(1, 2 * NT):
         whole = whole + s_t[p]
     total_sq = jnp.sum(whole, axis=1, keepdims=True)
     step = 0.5 / jnp.sqrt(total_sq * (1.0 / (2.0 * RANK * D)) + 1e-06)
-    arrived(8, grads.at[0])
+    arrived(11, grads.at[0])
     for p in range(NY):
         cols = slice(p * SIZE, (p + 1) * SIZE)
         nd_v[:, cols] = fd_v[:, cols] - grads[0, p] * step
         nu_v[:, cols] = fu_v[:, cols] - grads[1, p] * step
     for phase, size in drains:
         remote(size, size, send_sem.at[phase], recv_sem.at[phase], sibling).wait_send()
+
+    @pl.when(c == 0)
+    def _():
+        remote(r_buf, x_buf, send_sem.at[7], recv_sem.at[7], sibling).wait_send()
 
 
 def hand_over(*refs):
@@ -384,19 +407,21 @@
             vmem((ROWS * GROUP, SIZE), F32),
             vmem((ROWS, WIDTH), BF),
             vmem((2, NY, ROWS, SIZE), F32),
-            vmem((NT, 104, SIZE), F32),
+            vmem((NT, 64, SIZE), F32),
+            vmem((NT, 40, SIZE), F32),
             vmem((NYC, ROWS, SIZE), F32),
             vmem((NYC, ROWS, SIZE), F32),
-            vmem((2, 24, SIZE), F32),
+            vmem((NYC, 16, SIZE), F32),
             vmem((NYC, 24, SIZE), F32),
+            vmem((2, 256, SIZE), F32),
             vmem((NZ, 1, SIZE), F32),
             vmem((NZ, RANK, SIZE), F32),
             vmem((2, NY, RANK, SIZE), F32),
             vmem((2 * NT, 1, SIZE), F32),
             vmem((NY, 1, SIZE), F32),
             dma((len(inputs),)),
-            dma((10,)),
-            dma((10,)),
+            dma((13,)),
+            dma((13,)),
             dma((NY,)),
         ]
     )
@@ -419,6 +444,7 @@
             in_specs=[pl.BlockSpec(memory_space=vmem)] * len(outs),
             out_specs=tuple([anywhere] * len(outs)),
             scratch_shapes=[dma((len(outs),))],
+            compiler_params=pltpu.CompilerParams(vmem_limit_bytes=4 * 1024 * 1024),
             name="hand_over",
         )(*results)
     )

time: 51.1 us -> 46.4 us (0.908)
  local copies, waits for them, and re-layouts: 2.63 us -> 0 us
  Pallas kernels: 47 us -> 44.9 us
    unnamed x8 -> x0, local copies, waits for them, and re-layouts: 2.63 us -> none
    pallas_call x1, Pallas kernels: 1.96 us -> 0.86 us  [local(): pl.pallas_call(hand_over, out_shape=outs, in_specs=[pl.BlockSpec(memory_s...]
    pallas_call x1, Pallas kernels: 45.1 us -> 44.1 us  [local(): pl.pallas_call(kernel, out_shape=tuple((vmem(a.shape, a.dtype) for a in o...]
where the time goes in v4:
time: 46.4 us; the launch traced here: 46.2 us
  Pallas kernels  44.9 us (97%)
  between operations  1.29 us (3%)
    pallas_call x1, Pallas kernels, local(): pl.pallas_call(kernel, out_shape=tuple((vmem(a.shape, a.dtype) for a in o...  44.1 us

profile of v4, /device:TPU:1, one launch (start us, length us, event | category | flops | bytes accessed | tf_op | source)
XLA Modules:
  0.0 46.2 jit_solution(14548322364798252747)
XLA Ops:
  1.3 44.1 %decode_and_draft.1 = (bf16[32,1024]{1,0:T(8,128)(2,1)S(1)}, bf16[32,1024]{1,0:T(8,128)(2,1)S(1)}, f32[64,1024]{1,0:T(8,128)S(1)}, f32[64,1024]{1,0:T(8,128)S(1)}) custom-call(bf16[32,1024]{1,0:T(8,128)(2,1)} %q_hbm.1, bf16[32,128,128]{2,1,0:T(8,128)(2,1)} %bitcast.6, bf16[32,128,128]{2,1,0:T(8,128)(2,1)} %bitcast.7, bf16[32,128]{1,0:T(8,128)(2,1)} %nk_hbm.1, ...), custom_call_target="tpu_custom_call" | custom-call | tf_op jit(solution)/shard_map/decode_and_draft/pallas_call | solution.py:429
  45.4 0.9 %hand_over.1 = (bf16[32,1024]{1,0:T(8,128)(2,1)}, bf16[32,1024]{1,0:T(8,128)(2,1)}, f32[64,1024]{1,0:T(8,128)}, f32[64,1024]{1,0:T(8,128)}) custom-call(bf16[32,1024]{1,0:T(8,128)(2,1)S(1)} %get-tuple-element.8.refs_0_, bf16[32,1024]{1,0:T(8,128)(2,1)S(1)} %get-tuple-element.9.refs_1_, f32[64,1024]{1,0:T(8,128)S(1)} %get-tuple-element.10.refs_2_, ...), custom_call_target="tpu_custom_call" | custom-call | tf_op jit(solution)/shard_map/hand_over/pallas_call | solution.py:441

commit v5 on v4

--- a/solution.py
+++ b/solution.py
@@ -54,7 +54,7 @@
     hid_v, dn_v, nd_v, nu_v,
     q_v, ck_v, cv_v, nk_v, nv_v, len_v, res_v, gain_v, dr_v, tr_v, fd_v, fu_v,
     w_b, q3, ctx3, fg_b,
-    slices, e_buf, f_buf, r_buf, x_buf, a_buf, l_buf, base, c_buf, z_buf, grads, s_t, s_y,
+    slices, e_buf, u_buf, f_buf, h_buf, r_buf, x_buf, a_buf, l_buf, base, c_buf, z_buf, grads, s_t, s_y,
     in_sem, send_sem, recv_sem, slice_sem,
 ):
     r = lax.axis_index("replica")
@@ -100,14 +100,27 @@
         pltpu.make_async_copy(src, dst, in_sem.at[i])
         for i, (src, dst) in enumerate(
             (
-                (q_hbm, q_v), (nk_hbm, nk_v), (len_hbm, len_v), (tr_hbm, tr_v), (ck_hbm, ck_v), (fd_hbm, fd_v),
-                (fu_hbm, fu_v), (dr_hbm, dr_v), (cv_hbm, cv_v), (nv_hbm, nv_v), (res_hbm, res_v), (gain_hbm, gain_v),
+                (fd_hbm, fd_v), (fu_hbm, fu_v), (dr_hbm, dr_v), (q_hbm, q_v), (nk_hbm, nk_v), (len_hbm, len_v),
+                (tr_hbm, tr_v), (ck_hbm, ck_v), (cv_hbm, cv_v), (nv_hbm, nv_v), (res_hbm, res_v), (gain_hbm, gain_v),
             )
         )
     ]
     for load in loads:
         load.start()
-    for load in loads[:4]:
+    for load in loads[:3]:
+        load.wait()
+    low = iota((ROWS, SIZE), 1) < RANK
+    low16 = low[0:16]
+    w_b[0:RANK, :] = fd_v[...].astype(BF)
+    w_b[RANK:, :] = fu_v[...].astype(BF)
+    for g in range(GROUP):
+        slices[0, g] = dr_v[:, g * SIZE : (g + 1) * SIZE].astype(F32)
+    e_buf[t, 0:32, :] = dot_t(dr_v[...], w_b[...])
+    up_part = dot_t(w_b[RANK:, :], w_b[...])
+    up_half = jnp.where(c == 0, up_part[0:32], up_part[32:64])
+    e_buf[t, 32:48, :] = jnp.where(low16, pltpu.roll(up_half[0:16], RANK, 1), up_half[16:32])
+
+    for load in loads[3:7]:
         load.wait()
     for g in range(GROUP):
         q3[pl.ds(g, ROWS, stride=GROUP), :] = q_v[:, g * SIZE : (g + 1) * SIZE].astype(F32)
@@ -119,7 +132,9 @@
     queries = q3[...]
     scale = 1.0 / math.sqrt(SIZE)
     own_score = jnp.sum(queries * own_key, axis=1, keepdims=True) * scale
-    loads[4].wait()
+    onehot = (iota((1, SIZE), 1) == tr_v[...] + 64).astype(F32)
+    c_buf[z] = onehot
+    loads[7].wait()
     scores = lax.dot_general(
         queries.reshape(ROWS, GROUP, SIZE).astype(BF),
         ck_v[...],
@@ -127,18 +142,27 @@
         preferred_element_type=F32,
     ).reshape(ROWS * GROUP, SIZE)
 
-    for load in loads[5:8]:
-        load.wait()
-    low = iota((ROWS, SIZE), 1) < RANK
-    w_b[0:RANK, :] = fd_v[...].astype(BF)
-    w_b[RANK:, :] = fu_v[...].astype(BF)
-    for g in range(GROUP):
-        slices[0, g] = dr_v[:, g * SIZE : (g + 1) * SIZE].astype(F32)
-    e_buf[t, 0:32, :] = dot_t(dr_v[...], w_b[...])
-    up_part = dot_t(w_b[RANK:, :], w_b[...])
-    e_buf[t, 32:64, :] = jnp.where(low, pltpu.roll(up_part[0:32], RANK, 1), up_part[32:64])
-    onehot = (iota((1, SIZE), 1) == tr_v[...] + 64).astype(F32)
-    c_buf[z] = onehot
+    pl.semaphore_wait(barrier, len(everyone))
+    drains = []
+
+    def start(phase, src, dst, device):
+        remote(src, dst, send_sem.at[phase], recv_sem.at[phase], device).start()
+
+    def spread_to(phase, devices, src, size):
+        for device in devices:
+            start(phase, src, src, device)
+        drains.append((phase, size))
+
+    def arrived(phase, size):
+        remote(size, size, send_sem.at[phase], recv_sem.at[phase], sibling).wait_recv()
+
+    e_size = e_buf.at[pl.ds(0, NT - 1)]
+    f_size = f_buf.at[pl.ds(0, NT - 1), pl.ds(0, 17)]
+    c_size = c_buf.at[pl.ds(0, NZ - 1)]
+    r_size = r_buf.at[pl.ds(0, NYC - 1)]
+    spread_to(0, [at_t(p) for p in t_peers], e_buf.at[t], e_size)
+    for p in y_peers:
+        start(2, slices.at[0, p], r_buf.at[yc], at_yc(p * 2))
 
     live = iota((ROWS * GROUP, SIZE), 1).astype(F32) < lengths
     scores = jnp.where(live, scores * scale, -jnp.inf)
@@ -148,29 +172,6 @@
     total = jnp.sum(weights, axis=1, keepdims=True) + own_weight
     probs = (weights / total).astype(BF)
     own_prob = (own_weight / total).astype(BF).astype(F32)
-
-    pl.semaphore_wait(barrier, len(everyone))
-    drains = []
-
-    def start(phase, src, dst, device):
-        remote(src, dst, send_sem.at[phase], recv_sem.at[phase], device).start()
-
-    def spread_to(phase, devices, src, size):
-        for device in devices:
-            start(phase, src, src, device)
-        drains.append((phase, size))
-
-    def arrived(phase, size):
-        remote(size, size, send_sem.at[phase], recv_sem.at[phase], sibling).wait_recv()
-
-    e_size = e_buf.at[pl.ds(0, NT - 1)]
-    f_size = f_buf.at[pl.ds(0, NT - 1), pl.ds(0, 33)]
-    c_size = c_buf.at[pl.ds(0, NZ - 1)]
-    r_size = r_buf.at[pl.ds(0, NYC - 1)]
-    spread_to(0, [at_t(p) for p in t_peers], e_buf.at[t], e_size)
-    spread_to(1, [at_z(p) for p in z_peers], c_buf.at[z], c_size)
-    for p in y_peers:
-        start(2, slices.at[0, p], r_buf.at[yc], at_yc(p * 2))
 
     for load in loads[8:]:
         load.wait()
@@ -195,9 +196,11 @@
     eye = iota((ROWS, SIZE), 0) == iota((ROWS, SIZE), 1)
     square_row = jnp.sum(jnp.where(eye, square_col, 0.0), axis=0, keepdims=True)
     feature_part = dot_t(fg_b[...], w_b[...])
-    f_buf[t, 0:32, :] = feature_part
-    f_buf[t, 32:33, :] = square_row
-    spread_to(3, [at_t(p) for p in t_peers], f_buf.at[t, pl.ds(0, 33)], f_size)
+    f_buf[t, 0:16, :] = jnp.where(low16, pltpu.roll(feature_part[0:16], RANK, 1), feature_part[16:32])
+    f_buf[t, 16:17, :] = square_row
+    h_buf[t] = jnp.where(low16, feature_part[0:16], pltpu.roll(feature_part[16:32], RANK, 1))
+    spread_to(3, [at_t(p) for p in t_peers], f_buf.at[t, pl.ds(0, 17)], f_size)
+    spread_to(1, [at_z(p) for p in z_peers], c_buf.at[z], c_size)
     for p in y_peers:
         start(2, slices.at[1, p], r_buf.at[yc], at_yc(p * 2 + 1))
     start(2, slices.at[1 - c, y], r_buf.at[yc], sibling)
@@ -205,31 +208,28 @@
     r_buf[yc] = slices[c, y]
 
     arrived(0, e_size)
-    early = e_buf[0]
-    for p in range(1, NT):
-        early = early + e_buf[p]
-    low16 = low[0:16]
-    adapter = (early[0:32] * ROOT).astype(BF).astype(F32)
+    u_buf[c] = sum((e_buf[p, 32:48, :] for p in range(1, NT)), e_buf[0, 32:48, :])
+    spread_to(13, [sibling], u_buf.at[c], u_buf.at[0])
+    early = sum((e_buf[p, 0:32, :] for p in range(1, NT)), e_buf[0, 0:32, :])
+    adapter = (early * ROOT).astype(BF).astype(F32)
     a_buf[yc] = jnp.where(low16, adapter[0:16], pltpu.roll(adapter[16:32], RANK, 1))
     for p in y_peers:
         start(4, a_buf.at[yc], a_buf.at[yc], at_yc(p * 2 + 1))
     start(4, a_buf.at[yc], a_buf.at[yc], sibling)
     drains.append((4, a_buf.at[pl.ds(0, NY)]))
-    ups = early[32:64]
-    upper = jnp.dot(adapter[:, 0:32], ups, precision=EXACT, preferred_element_type=F32)
-    lower = jnp.dot(pltpu.roll(adapter, 96, 1)[:, 0:32], ups, precision=EXACT, preferred_element_type=F32)
-    ahead = early[0:32] + COEF * (pltpu.roll(upper, RANK, 1) + lower)
+    arrived(13, u_buf.at[0])
+    ups = jnp.concatenate([pltpu.roll(u_buf[0], RANK, 1), u_buf[0], pltpu.roll(u_buf[1], RANK, 1), u_buf[1]], axis=0)
+    spread = jnp.dot(adapter[:, 0:RANK], ups, precision=EXACT, preferred_element_type=F32)
+    ahead = early + COEF * spread
+    ahead = jnp.where(low16, pltpu.roll(ahead[0:16], RANK, 1), ahead[16:32])
     arrived(1, c_size)
     counts = c_buf[0] + c_buf[1] + c_buf[2] + c_buf[3]
     marks = onehot + pltpu.roll(counts, 32, 1)
     arrived(3, f_size)
-    summed = f_buf[0, 0:33, :]
-    for p in range(1, NT):
-        summed = summed + f_buf[p, 0:33, :]
-    rs_row = lax.rsqrt(summed[32:33] * (1.0 / D) + 1e-05)
+    summed = sum((f_buf[p, 0:17, :] for p in range(1, NT)), f_buf[0, 0:17, :])
+    rs_row = lax.rsqrt(summed[16:17] * (1.0 / D) + 1e-05)
     rs_col = jnp.sum(jnp.where(eye, rs_row, 0.0), axis=1, keepdims=True)
-    back = COEF * (ahead - rs_col * summed[0:32])
-    l_buf[yc, 0:16, :] = jnp.where(low16, pltpu.roll(back[0:16], RANK, 1), back[16:32])
+    l_buf[yc, 0:16, :] = COEF * (ahead - jnp.where(low16, rs_col[0:16], rs_col[16:32]) * summed[0:16])
     l_buf[yc, 16:17, :] = jnp.where(iota((1, SIZE), 1) < ROWS, rs_row, 0.0) + marks
     l_mine = l_buf.at[yc, pl.ds(0, 17)]
     l_row = l_buf.at[yc, pl.ds(16, 1)]
@@ -246,13 +246,7 @@
     def _():
         start(7, r_buf, x_buf, sibling)
 
-    serve = (summed[0:32] * rs_col * ROOT).astype(BF)
-    drafted = jnp.dot(serve[:, 0:RANK], w_b[RANK:, :], preferred_element_type=F32)
-    for g in range(GROUP):
-        cols = slice(g * SIZE, (g + 1) * SIZE)
-        hidden = (slices[1, g] * rs_col).astype(BF)
-        hid_v[:, cols] = hidden
-        dn_v[:, cols] = (hidden.astype(F32) + COEF * drafted[:, cols]).astype(BF)
+    spread_to(14, [at_t(p) for p in t_peers], h_buf.at[t], h_buf.at[pl.ds(0, NT - 1)])
 
     @pl.when(c == 0)
     def _():
@@ -273,18 +267,15 @@
         arrived(5, l_buf.at[0, pl.ds(0, 17)])
         arrived(6, l_buf.at[pl.ds(0, NYC - 2), pl.ds(16, 1)])
 
-    tiles = l_buf[:, 16:24, :]
-    tiles = jnp.where(iota((NYC, 8, SIZE), 1) == 0, tiles, 0.0)
-    lane = iota((256, SIZE), 1)
-    load_all = pltpu.roll(jnp.sum(jnp.sum(tiles, axis=0), axis=0, keepdims=True), 96, 1)
+    rows_of = jnp.broadcast_to(l_buf[:, 16:17, :], (NYC, 16, SIZE))
+    lane = iota((NYC, 16, SIZE), 2)
+    load_all = pltpu.roll(jnp.sum(l_buf[:, 16:17, :], axis=0), 96, 1)
     load_all = jnp.where(iota((1, SIZE), 1) // 16 == 4, load_all, 0.0)
-    own_row = (lane == (iota((256, SIZE), 0) // 16) * 8).astype(F32)
-    extras = jnp.dot(own_row, tiles.reshape(SIZE, SIZE), precision=EXACT, preferred_element_type=F32)
-    weight = 1.0 / (ROWS * jnp.sum(extras * load_all, axis=1, keepdims=True))
+    weight = 1.0 / (ROWS * jnp.sum(rows_of * load_all[None], axis=2, keepdims=True))
 
     @pl.when(c == 0)
     def _():
-        left = (l_buf[:, 0:16, :].reshape(256, SIZE) * weight).astype(BF)
+        left = (l_buf[:, 0:16, :] * weight).reshape(256, SIZE).astype(BF)
         top_rows = r_buf[:, 0:16, :].reshape(256, SIZE).astype(BF)
         bottom_rows = r_buf[:, 16:32, :].reshape(256, SIZE).astype(BF)
         z_buf[z] = (dot_rows(left, top_rows)[0:RANK] + dot_rows(left, bottom_rows)[RANK:]) * ROOT
@@ -292,17 +283,28 @@
     @pl.when(c == 1)
     def _():
         left = a_buf[...].reshape(256, SIZE).astype(BF)
-        place = lax.rem(iota((256, SIZE), 0), 16)
+        place = iota((NYC, 16, SIZE), 1)
 
         def half(h):
-            rs = jnp.sum(jnp.where(lane == place + 16 * h, extras, 0.0), axis=1, keepdims=True)
-            gained = r_buf[:, 16 * h : 16 * h + 16, :].reshape(256, SIZE)
-            return dot_rows(left, (weight * (base[h] - rs * gained)).astype(BF))
+            rs = jnp.sum(jnp.where(lane == place + 16 * h, rows_of, 0.0), axis=2, keepdims=True)
+            resid = weight * (base[h].reshape(NYC, 16, SIZE) - rs * r_buf[:, 16 * h : 16 * h + 16, :])
+            return dot_rows(left, resid.reshape(256, SIZE).astype(BF))
 
         z_buf[z] = (half(0)[0:RANK] + half(1)[RANK:]) * COEF
 
     z_size = z_buf.at[pl.ds(0, NZ - 1)]
     spread_to(8, [at_z(p) for p in z_peers], z_buf.at[z], z_size)
+    arrived(14, h_buf.at[pl.ds(0, NT - 1)])
+    served = sum((h_buf[p] for p in range(1, NT)), h_buf[0])
+    served = jnp.concatenate([served, pltpu.roll(served, RANK, 1)], axis=0)
+    serve = (served * rs_col * ROOT).astype(BF)
+    drafted = jnp.dot(serve[:, 0:RANK], w_b[RANK:, :], preferred_element_type=F32)
+    for g in range(GROUP):
+        cols = slice(g * SIZE, (g + 1) * SIZE)
+        hidden = (slices[1, g] * rs_col).astype(BF)
+        hid_v[:, cols] = hidden
+        dn_v[:, cols] = (hidden.astype(F32) + COEF * drafted[:, cols]).astype(BF)
+
     arrived(8, z_size)
     grad = z_buf[0] + z_buf[1] + z_buf[2] + z_buf[3]
     grads[c, y] = grad
@@ -407,8 +409,10 @@
             vmem((ROWS * GROUP, SIZE), F32),
             vmem((ROWS, WIDTH), BF),
             vmem((2, NY, ROWS, SIZE), F32),
-            vmem((NT, 64, SIZE), F32),
-            vmem((NT, 40, SIZE), F32),
+            vmem((NT, 48, SIZE), F32),
+            vmem((2, 16, SIZE), F32),
+            vmem((NT, 24, SIZE), F32),
+            vmem((NT, 16, SIZE), F32),
             vmem((NYC, ROWS, SIZE), F32),
             vmem((NYC, ROWS, SIZE), F32),
             vmem((NYC, 16, SIZE), F32),
@@ -420,8 +424,8 @@
             vmem((2 * NT, 1, SIZE), F32),
             vmem((NY, 1, SIZE), F32),
             dma((len(inputs),)),
-            dma((13,)),
-            dma((13,)),
+            dma((15,)),
+            dma((15,)),
             dma((NY,)),
         ]
     )

time: 46.4 us -> 45.8 us (0.987)
  Pallas kernels: 44.9 us -> 44.3 us
    pallas_call x1, Pallas kernels: 44.1 us -> 43.5 us  [local(): pl.pallas_call(kernel, out_shape=tuple((vmem(a.shape, a.dtype) for a in o...]
where the time goes in v5:
time: 45.8 us; the launch traced here: 45.6 us
  Pallas kernels  44.3 us (97%)
  between operations  1.29 us (3%)
    pallas_call x1, Pallas kernels, local(): pl.pallas_call(kernel, out_shape=tuple((vmem(a.shape, a.dtype) for a in o...  43.5 us

profile of v5, /device:TPU:1, one launch (start us, length us, event | category | flops | bytes accessed | tf_op | source)
XLA Modules:
  0.0 45.6 jit_solution(3866001081530321227)
XLA Ops:
  1.3 43.5 %decode_and_draft.1 = (bf16[32,1024]{1,0:T(8,128)(2,1)S(1)}, bf16[32,1024]{1,0:T(8,128)(2,1)S(1)}, f32[64,1024]{1,0:T(8,128)S(1)}, f32[64,1024]{1,0:T(8,128)S(1)}) custom-call(bf16[32,1024]{1,0:T(8,128)(2,1)} %q_hbm.1, bf16[32,128,128]{2,1,0:T(8,128)(2,1)} %bitcast.6, bf16[32,128,128]{2,1,0:T(8,128)(2,1)} %bitcast.7, bf16[32,128]{1,0:T(8,128)(2,1)} %nk_hbm.1, ...), custom_call_target="tpu_custom_call" | custom-call | tf_op jit(solution)/shard_map/decode_and_draft/pallas_call | solution.py:433
  44.8 0.9 %hand_over.1 = (bf16[32,1024]{1,0:T(8,128)(2,1)}, bf16[32,1024]{1,0:T(8,128)(2,1)}, f32[64,1024]{1,0:T(8,128)}, f32[64,1024]{1,0:T(8,128)}) custom-call(bf16[32,1024]{1,0:T(8,128)(2,1)S(1)} %get-tuple-element.8.refs_0_, bf16[32,1024]{1,0:T(8,128)(2,1)S(1)} %get-tuple-element.9.refs_1_, f32[64,1024]{1,0:T(8,128)S(1)} %get-tuple-element.10.refs_2_, ...), custom_call_target="tpu_custom_call" | custom-call | tf_op jit(solution)/shard_map/hand_over/pallas_call | solution.py:445

commit v6 on v5

--- a/solution.py
+++ b/solution.py
@@ -120,6 +120,31 @@
     up_half = jnp.where(c == 0, up_part[0:32], up_part[32:64])
     e_buf[t, 32:48, :] = jnp.where(low16, pltpu.roll(up_half[0:16], RANK, 1), up_half[16:32])
 
+    pl.semaphore_wait(barrier, len(everyone))
+    drains = []
+
+    def start(phase, src, dst, device):
+        remote(src, dst, send_sem.at[phase], recv_sem.at[phase], device).start()
+
+    def spread_to(phase, devices, src, size):
+        for device in devices:
+            start(phase, src, src, device)
+        drains.append((phase, size))
+
+    def sent():
+        for phase, size in drains:
+            remote(size, size, send_sem.at[phase], recv_sem.at[phase], sibling).wait_send()
+        drains.clear()
+
+    def arrived(phase, size):
+        remote(size, size, send_sem.at[phase], recv_sem.at[phase], sibling).wait_recv()
+
+    e_size = e_buf.at[pl.ds(0, NT - 1)]
+    f_size = f_buf.at[pl.ds(0, NT - 1), pl.ds(0, 17)]
+    c_size = c_buf.at[pl.ds(0, NZ - 1)]
+    r_size = r_buf.at[pl.ds(0, NYC - 1)]
+    spread_to(0, [at_t(p) for p in t_peers], e_buf.at[t], e_size)
+
     for load in loads[3:7]:
         load.wait()
     for g in range(GROUP):
@@ -141,28 +166,6 @@
         (((2,), (2,)), ((0,), (0,))),
         preferred_element_type=F32,
     ).reshape(ROWS * GROUP, SIZE)
-
-    pl.semaphore_wait(barrier, len(everyone))
-    drains = []
-
-    def start(phase, src, dst, device):
-        remote(src, dst, send_sem.at[phase], recv_sem.at[phase], device).start()
-
-    def spread_to(phase, devices, src, size):
-        for device in devices:
-            start(phase, src, src, device)
-        drains.append((phase, size))
-
-    def arrived(phase, size):
-        remote(size, size, send_sem.at[phase], recv_sem.at[phase], sibling).wait_recv()
-
-    e_size = e_buf.at[pl.ds(0, NT - 1)]
-    f_size = f_buf.at[pl.ds(0, NT - 1), pl.ds(0, 17)]
-    c_size = c_buf.at[pl.ds(0, NZ - 1)]
-    r_size = r_buf.at[pl.ds(0, NYC - 1)]
-    spread_to(0, [at_t(p) for p in t_peers], e_buf.at[t], e_size)
-    for p in y_peers:
-        start(2, slices.at[0, p], r_buf.at[yc], at_yc(p * 2))
 
     live = iota((ROWS * GROUP, SIZE), 1).astype(F32) < lengths
     scores = jnp.where(live, scores * scale, -jnp.inf)
@@ -201,6 +204,8 @@
     h_buf[t] = jnp.where(low16, feature_part[0:16], pltpu.roll(feature_part[16:32], RANK, 1))
     spread_to(3, [at_t(p) for p in t_peers], f_buf.at[t, pl.ds(0, 17)], f_size)
     spread_to(1, [at_z(p) for p in z_peers], c_buf.at[z], c_size)
+    for p in y_peers:
+        start(2, slices.at[0, p], r_buf.at[yc], at_yc(p * 2))
     for p in y_peers:
         start(2, slices.at[1, p], r_buf.at[yc], at_yc(p * 2 + 1))
     start(2, slices.at[1 - c, y], r_buf.at[yc], sibling)
@@ -305,6 +310,12 @@
         hid_v[:, cols] = hidden
         dn_v[:, cols] = (hidden.astype(F32) + COEF * drafted[:, cols]).astype(BF)
 
+
+    @pl.when(c == 0)
+    def _():
+        remote(r_buf, x_buf, send_sem.at[7], recv_sem.at[7], sibling).wait_send()
+
+    sent()
     arrived(8, z_size)
     grad = z_buf[0] + z_buf[1] + z_buf[2] + z_buf[3]
     grads[c, y] = grad
@@ -343,17 +354,33 @@
         whole = whole + s_t[p]
     total_sq = jnp.sum(whole, axis=1, keepdims=True)
     step = 0.5 / jnp.sqrt(total_sq * (1.0 / (2.0 * RANK * D)) + 1e-06)
+    @pl.when(c == 0)
+    def _():
+        for p in range(NY):
+            cols = slice(p * SIZE, (p + 1) * SIZE)
+            nd_v[:, cols] = fd_v[:, cols] - grads[0, p] * step
+
+    @pl.when(c == 1)
+    def _():
+        for p in range(NY):
+            cols = slice(p * SIZE, (p + 1) * SIZE)
+            nu_v[:, cols] = fu_v[:, cols] - grads[1, p] * step
+
     arrived(11, grads.at[0])
-    for p in range(NY):
-        cols = slice(p * SIZE, (p + 1) * SIZE)
-        nd_v[:, cols] = fd_v[:, cols] - grads[0, p] * step
-        nu_v[:, cols] = fu_v[:, cols] - grads[1, p] * step
-    for phase, size in drains:
-        remote(size, size, send_sem.at[phase], recv_sem.at[phase], sibling).wait_send()
 
     @pl.when(c == 0)
     def _():
-        remote(r_buf, x_buf, send_sem.at[7], recv_sem.at[7], sibling).wait_send()
+        for p in range(NY):
+            cols = slice(p * SIZE, (p + 1) * SIZE)
+            nu_v[:, cols] = fu_v[:, cols] - grads[1, p] * step
+
+    @pl.when(c == 1)
+    def _():
+        for p in range(NY):
+            cols = slice(p * SIZE, (p + 1) * SIZE)
+            nd_v[:, cols] = fd_v[:, cols] - grads[0, p] * step
+
+    sent()
 
 
 def hand_over(*refs):

time: 45.8 us -> 47.5 us (1.037)
  Pallas kernels: 44.3 us -> 46 us
    pallas_call x1, Pallas kernels: 43.5 us -> 45.2 us  [local(): pl.pallas_call(kernel, out_shape=tuple((vmem(a.shape, a.dtype) for a in o...]
where the time goes in v6:
time: 47.5 us; the launch traced here: 47.3 us
  Pallas kernels  46 us (97%)
  between operations  1.29 us (3%)
    pallas_call x1, Pallas kernels, local(): pl.pallas_call(kernel, out_shape=tuple((vmem(a.shape, a.dtype) for a in o...  45.2 us

profile of v6, /device:TPU:1, one launch (start us, length us, event | category | flops | bytes accessed | tf_op | source)
XLA Modules:
  0.0 47.3 jit_solution(13300669042600138931)
XLA Ops:
  1.3 45.2 %decode_and_draft.1 = (bf16[32,1024]{1,0:T(8,128)(2,1)S(1)}, bf16[32,1024]{1,0:T(8,128)(2,1)S(1)}, f32[64,1024]{1,0:T(8,128)S(1)}, f32[64,1024]{1,0:T(8,128)S(1)}) custom-call(bf16[32,1024]{1,0:T(8,128)(2,1)} %q_hbm.1, bf16[32,128,128]{2,1,0:T(8,128)(2,1)} %bitcast.6, bf16[32,128,128]{2,1,0:T(8,128)(2,1)} %bitcast.7, bf16[32,128]{1,0:T(8,128)(2,1)} %nk_hbm.1, ...), custom_call_target="tpu_custom_call" | custom-call | tf_op jit(solution)/shard_map/decode_and_draft/pallas_call | solution.py:460
  46.5 0.9 %hand_over.1 = (bf16[32,1024]{1,0:T(8,128)(2,1)}, bf16[32,1024]{1,0:T(8,128)(2,1)}, f32[64,1024]{1,0:T(8,128)}, f32[64,1024]{1,0:T(8,128)}) custom-call(bf16[32,1024]{1,0:T(8,128)(2,1)S(1)} %get-tuple-element.8.refs_0_, bf16[32,1024]{1,0:T(8,128)(2,1)S(1)} %get-tuple-element.9.refs_1_, f32[64,1024]{1,0:T(8,128)S(1)} %get-tuple-element.10.refs_2_, ...), custom_call_target="tpu_custom_call" | custom-call | tf_op jit(solution)/shard_map/hand_over/pallas_call | solution.py:472

commit v7 on v5

--- a/solution.py
+++ b/solution.py
@@ -153,6 +153,11 @@
             start(phase, src, src, device)
         drains.append((phase, size))
 
+    def sent():
+        for phase, size in drains:
+            remote(size, size, send_sem.at[phase], recv_sem.at[phase], sibling).wait_send()
+        drains.clear()
+
     def arrived(phase, size):
         remote(size, size, send_sem.at[phase], recv_sem.at[phase], sibling).wait_recv()
 
@@ -160,6 +165,7 @@
     f_size = f_buf.at[pl.ds(0, NT - 1), pl.ds(0, 17)]
     c_size = c_buf.at[pl.ds(0, NZ - 1)]
     r_size = r_buf.at[pl.ds(0, NYC - 1)]
+    spread_to(1, [at_z(p) for p in z_peers], c_buf.at[z], c_size)
     spread_to(0, [at_t(p) for p in t_peers], e_buf.at[t], e_size)
     for p in y_peers:
         start(2, slices.at[0, p], r_buf.at[yc], at_yc(p * 2))
@@ -200,7 +206,6 @@
     f_buf[t, 16:17, :] = square_row
     h_buf[t] = jnp.where(low16, feature_part[0:16], pltpu.roll(feature_part[16:32], RANK, 1))
     spread_to(3, [at_t(p) for p in t_peers], f_buf.at[t, pl.ds(0, 17)], f_size)
-    spread_to(1, [at_z(p) for p in z_peers], c_buf.at[z], c_size)
     for p in y_peers:
         start(2, slices.at[1, p], r_buf.at[yc], at_yc(p * 2 + 1))
     start(2, slices.at[1 - c, y], r_buf.at[yc], sibling)
@@ -305,6 +310,12 @@
         hid_v[:, cols] = hidden
         dn_v[:, cols] = (hidden.astype(F32) + COEF * drafted[:, cols]).astype(BF)
 
+
+    @pl.when(c == 0)
+    def _():
+        remote(r_buf, x_buf, send_sem.at[7], recv_sem.at[7], sibling).wait_send()
+
+    sent()
     arrived(8, z_size)
     grad = z_buf[0] + z_buf[1] + z_buf[2] + z_buf[3]
     grads[c, y] = grad
@@ -343,17 +354,33 @@
         whole = whole + s_t[p]
     total_sq = jnp.sum(whole, axis=1, keepdims=True)
     step = 0.5 / jnp.sqrt(total_sq * (1.0 / (2.0 * RANK * D)) + 1e-06)
+    @pl.when(c == 0)
+    def _():
+        for p in range(NY):
+            cols = slice(p * SIZE, (p + 1) * SIZE)
+            nd_v[:, cols] = fd_v[:, cols] - grads[0, p] * step
+
+    @pl.when(c == 1)
+    def _():
+        for p in range(NY):
+            cols = slice(p * SIZE, (p + 1) * SIZE)
+            nu_v[:, cols] = fu_v[:, cols] - grads[1, p] * step
+
     arrived(11, grads.at[0])
-    for p in range(NY):
-        cols = slice(p * SIZE, (p + 1) * SIZE)
-        nd_v[:, cols] = fd_v[:, cols] - grads[0, p] * step
-        nu_v[:, cols] = fu_v[:, cols] - grads[1, p] * step
-    for phase, size in drains:
-        remote(size, size, send_sem.at[phase], recv_sem.at[phase], sibling).wait_send()
 
     @pl.when(c == 0)
     def _():
-        remote(r_buf, x_buf, send_sem.at[7], recv_sem.at[7], sibling).wait_send()
+        for p in range(NY):
+            cols = slice(p * SIZE, (p + 1) * SIZE)
+            nu_v[:, cols] = fu_v[:, cols] - grads[1, p] * step
+
+    @pl.when(c == 1)
+    def _():
+        for p in range(NY):
+            cols = slice(p * SIZE, (p + 1) * SIZE)
+            nd_v[:, cols] = fd_v[:, cols] - grads[0, p] * step
+
+    sent()
 
 
 def hand_over(*refs):

time: 45.8 us -> 45.8 us (level)
  no operation moved by 1% of the time
where the time goes in v7:
time: 45.8 us; the launch traced here: 45.7 us
  Pallas kernels  44.4 us (97%)
  between operations  1.29 us (3%)
    pallas_call x1, Pallas kernels, local(): pl.pallas_call(kernel, out_shape=tuple((vmem(a.shape, a.dtype) for a in o...  43.6 us

profile of v7, /device:TPU:1, one launch (start us, length us, event | category | flops | bytes accessed | tf_op | source)
XLA Modules:
  0.0 45.7 jit_solution(1775005355590281628)
XLA Ops:
  1.3 43.6 %decode_and_draft.1 = (bf16[32,1024]{1,0:T(8,128)(2,1)S(1)}, bf16[32,1024]{1,0:T(8,128)(2,1)S(1)}, f32[64,1024]{1,0:T(8,128)S(1)}, f32[64,1024]{1,0:T(8,128)S(1)}) custom-call(bf16[32,1024]{1,0:T(8,128)(2,1)} %q_hbm.1, bf16[32,128,128]{2,1,0:T(8,128)(2,1)} %bitcast.6, bf16[32,128,128]{2,1,0:T(8,128)(2,1)} %bitcast.7, bf16[32,128]{1,0:T(8,128)(2,1)} %nk_hbm.1, ...), custom_call_target="tpu_custom_call" | custom-call | tf_op jit(solution)/shard_map/decode_and_draft/pallas_call | solution.py:460
  44.8 0.9 %hand_over.1 = (bf16[32,1024]{1,0:T(8,128)(2,1)}, bf16[32,1024]{1,0:T(8,128)(2,1)}, f32[64,1024]{1,0:T(8,128)}, f32[64,1024]{1,0:T(8,128)}) custom-call(bf16[32,1024]{1,0:T(8,128)(2,1)S(1)} %get-tuple-element.8.refs_0_, bf16[32,1024]{1,0:T(8,128)(2,1)S(1)} %get-tuple-element.9.refs_1_, f32[64,1024]{1,0:T(8,128)S(1)} %get-tuple-element.10.refs_2_, ...), custom_call_target="tpu_custom_call" | custom-call | tf_op jit(solution)/shard_map/hand_over/pallas_call | solution.py:472

commit v8 on v7

--- a/solution.py
+++ b/solution.py
@@ -320,38 +320,38 @@
     grad = z_buf[0] + z_buf[1] + z_buf[2] + z_buf[3]
     grads[c, y] = grad
 
-    s_y[y] = jnp.sum(grad * grad, axis=0, keepdims=True)
+    place_t = t * 2 + c
+    s_t[place_t] = jnp.sum(grad * grad, axis=0, keepdims=True)
+    st_size = s_t.at[pl.ds(0, 2 * NT - 1)]
+    spread_to(
+        12,
+        [at_t(p) for p in t_peers] + [(z * NYC + y * 2 + 1 - c, p) for p in t_peers] + [sibling],
+        s_t.at[place_t],
+        st_size,
+    )
     own_core = [at_yc(p * 2 + c) for p in y_peers]
-    s_size = s_y.at[pl.ds(0, NY - 1)]
-    spread_to(9, own_core, s_y.at[y], s_size)
     mine = grads.at[c, y]
     for device in own_core:
         remote(mine, mine, send_sem.at[10], slice_sem.at[y], device).start()
     g_size = grads.at[0, pl.ds(0, NY - 1)]
     drains.append((10, g_size))
     start(11, mine, mine, sibling)
-    arrived(9, s_size)
-    part = s_y[0]
-    for p in range(1, NY):
-        part = part + s_y[p]
-    place_t = t * 2 + c
-    s_t[place_t] = part
-    st_size = s_t.at[pl.ds(0, 2 * NT - 1)]
-    spread_to(
-        12,
-        [at_t(p) for p in t_peers] + [(z * NYC + y * 2 + 1 - c, p) for p in t_peers] + [sibling],
-        s_t.at[place_t],
-        st_size,
-    )
+    arrived(12, st_size)
+    part = s_t[0]
+    for p in range(1, 2 * NT):
+        part = part + s_t[p]
+    s_y[y] = part
+    s_size = s_y.at[pl.ds(0, NY - 1)]
+    spread_to(9, own_core, s_y.at[y], s_size)
     for p in reversed(y_peers):
         piece = grads.at[c, p]
         remote(piece, piece, send_sem.at[10], slice_sem.at[p], sibling).wait_recv()
         start(11, piece, piece, sibling)
     drains.append((11, grads.at[0]))
-    arrived(12, st_size)
-    whole = s_t[0]
-    for p in range(1, 2 * NT):
-        whole = whole + s_t[p]
+    arrived(9, s_size)
+    whole = s_y[0]
+    for p in range(1, NY):
+        whole = whole + s_y[p]
     total_sq = jnp.sum(whole, axis=1, keepdims=True)
     step = 0.5 / jnp.sqrt(total_sq * (1.0 / (2.0 * RANK * D)) + 1e-06)
     @pl.when(c == 0)

time: 45.8 us -> 45.3 us (0.989)
  Pallas kernels: 44.4 us -> 43.9 us
    pallas_call x1, Pallas kernels: 43.6 us -> 43 us  [local(): pl.pallas_call(kernel, out_shape=tuple((vmem(a.shape, a.dtype) for a in o...]
where the time goes in v8:
time: 45.3 us; the launch traced here: 45.1 us
  Pallas kernels  43.9 us (97%)
  between operations  1.29 us (3%)
    pallas_call x1, Pallas kernels, local(): pl.pallas_call(kernel, out_shape=tuple((vmem(a.shape, a.dtype) for a in o...  43 us

profile of v8, /device:TPU:1, one launch (start us, length us, event | category | flops | bytes accessed | tf_op | source)
XLA Modules:
  0.0 45.1 jit_solution(12215074277513202852)
XLA Ops:
  1.3 43.0 %decode_and_draft.1 = (bf16[32,1024]{1,0:T(8,128)(2,1)S(1)}, bf16[32,1024]{1,0:T(8,128)(2,1)S(1)}, f32[64,1024]{1,0:T(8,128)S(1)}, f32[64,1024]{1,0:T(8,128)S(1)}) custom-call(bf16[32,1024]{1,0:T(8,128)(2,1)} %q_hbm.1, bf16[32,128,128]{2,1,0:T(8,128)(2,1)} %bitcast.6, bf16[32,128,128]{2,1,0:T(8,128)(2,1)} %bitcast.7, bf16[32,128]{1,0:T(8,128)(2,1)} %nk_hbm.1, ...), custom_call_target="tpu_custom_call" | custom-call | tf_op jit(solution)/shard_map/decode_and_draft/pallas_call | solution.py:460
  44.3 0.9 %hand_over.1 = (bf16[32,1024]{1,0:T(8,128)(2,1)}, bf16[32,1024]{1,0:T(8,128)(2,1)}, f32[64,1024]{1,0:T(8,128)}, f32[64,1024]{1,0:T(8,128)}) custom-call(bf16[32,1024]{1,0:T(8,128)(2,1)S(1)} %get-tuple-element.8.refs_0_, bf16[32,1024]{1,0:T(8,128)(2,1)S(1)} %get-tuple-element.9.refs_1_, f32[64,1024]{1,0:T(8,128)S(1)} %get-tuple-element.10.refs_2_, ...), custom_call_target="tpu_custom_call" | custom-call | tf_op jit(solution)/shard_map/hand_over/pallas_call | solution.py:472
